TPU v7x, 32 devices: a whole 2x2x4 slice. The times are simulated.
32 devices in a mesh: batch: 8 (over y, x, core), seq: 4 (over z).
Axes of the slice: x: 2, y: 2, z: 4, core: 2. Of those that a mesh axis runs over, the one named last changes fastest.
Arguments:
- tokens: bfloat16 [16, 1024, 1024], P('batch', 'seq'), may hold values from -6 to 6
- segment_ids: int32 [16, 1024], P('batch', 'seq'), may hold values from 0 to 3, as said below
- padding_mask: int32 [16, 1024], P('batch', 'seq'), may hold values from 0 to 1, as said below
- qkv_weight: bfloat16 [1024, 3072], P(('batch', 'seq')), may hold values from -0.1875 to 0.1875
- out_weight: bfloat16 [1024, 1024], P(('batch', 'seq')), may hold values from -1 to 1
- wide_weight: bfloat16 [1024, 5248], P(('batch', 'seq')), may hold values from -0.1875 to 0.1875
- narrow_weight: bfloat16 [1024, 2624], P(('batch', 'seq')), may hold values from -0.25 to 0.25
- first_gain: bfloat16 [1024], P(('batch', 'seq')), may hold values from 0.099609375 to 1.8984375
- second_gain: bfloat16 [1024], P(('batch', 'seq')), may hold values from 0.099609375 to 1.8984375
- cotangent: bfloat16 [16, 1024, 1024], P('batch', 'seq'), may hold values from -6 to 6
Outputs:
- outputs: bfloat16 [16, 1024, 1024], P('batch', 'seq')
- grad_tokens: bfloat16 [16, 1024, 1024], P('batch', 'seq')
- grad_qkv: float32 [1024, 3072], P(('batch', 'seq'))
- grad_out: float32 [1024, 1024], P(('batch', 'seq'))
- grad_wide: float32 [1024, 5248], P(('batch', 'seq'))
- grad_narrow: float32 [1024, 2624], P(('batch', 'seq'))
- grad_first_gain: float32 [1024], P(('batch', 'seq'))
- grad_second_gain: float32 [1024], P(('batch', 'seq'))
Inputs may be any that keep to these rules, and one draw needn't show every extreme that they name: `segment_ids`: in every sequence the document numbers start at 0, never fall, and rise by one where a new document begins; in each group of 2 sequences that share a batch index one sequence is a single document. `padding_mask`: Padding, where a sequence has any, fills its last positions, fewer than 129 of them; single-document sequences have none.
All inputs are finite; a program needn't handle non-finite values.
Results may differ from a plain program's by a relative error of at most 0.017.
Values may be sent and summed in bfloat16 or wider, within the bound.
A program may use at most 192 MiB of HBM per device.

v0:
```python
import jax
import jax.numpy as jnp
from jax import lax
from jax.sharding import PartitionSpec as P

HDIM = 64
FF = 2624
HALF = 64


NORM_EPS = 1e-05
MASK_FILL = -1e30
ROPE_BASE = 10000.0


def with_halo(array, sides, width):
    for axis, dim in sides:
        size, length = (lax.axis_size(axis), array.shape[dim])
        up = [(i, (i + 1) % size) for i in range(size - 1)]
        down = [(j, i) for i, j in up]
        last = lax.slice_in_dim(array, length - width, length, axis=dim)
        first = lax.slice_in_dim(array, 0, width, axis=dim)
        before = lax.ppermute(last, axis, up)
        after = lax.ppermute(first, axis, down)
        array = jnp.concatenate([before, array, after], axis=dim)
    return array


def norm_forward(values, norm_gain):
    center = values - jnp.mean(values, -1, keepdims=True)
    spread = jnp.mean(center * center, -1, keepdims=True)
    inverse = lax.rsqrt(spread + NORM_EPS)
    unit_part = center * inverse
    return (unit_part * norm_gain, unit_part, inverse)


def norm_backward(upstream, unit_part, inverse, norm_gain):
    scaled = upstream * norm_gain
    grad_gain = jnp.sum(upstream * unit_part, 0)
    grad_values = inverse * (
        scaled
        - jnp.mean(scaled, -1, keepdims=True)
        - unit_part * jnp.mean(scaled * unit_part, -1, keepdims=True)
    )
    return (grad_values, grad_gain)


def rope_angles(positions):
    half_dim = HDIM // 2
    frequency = ROPE_BASE ** (-(2.0 * jnp.arange(half_dim, dtype=jnp.float32)) / HDIM)
    return positions[:, None] * frequency[None, :]


def rotate(vectors, angles):
    half_dim = vectors.shape[-1] // 2
    cosine = jnp.cos(angles)[:, None, :]
    sine = jnp.sin(angles)[:, None, :]
    first_half = vectors[..., :half_dim]
    second_half = vectors[..., half_dim:]
    return jnp.concatenate(
        [first_half * cosine - second_half * sine, second_half * cosine + first_half * sine], -1
    )


def gated_unit(gate_in, gate_up):
    return jax.nn.gelu(gate_in, approximate=False) * gate_up


def band_scores(queries, key_rows, allowed):
    scores = jnp.einsum(
        "qhd,khd->hqk", queries, key_rows, preferred_element_type=jnp.float32
    ) * HDIM ** (-0.5)
    return jnp.where(allowed[None], scores, MASK_FILL)


def row_forward(entries):
    queries, key_rows, values, allowed = entries
    masked = band_scores(queries, key_rows, allowed)
    row_max = jnp.max(masked, -1, keepdims=True)
    weights = jnp.where(allowed[None], jnp.exp(masked - row_max), 0.0)
    totals = jnp.sum(weights, -1, keepdims=True)
    attn_probs = (weights / totals).astype(jnp.bfloat16)
    mixture = jnp.einsum("hqk,khd->qhd", attn_probs, values, preferred_element_type=jnp.float32)
    return (mixture.astype(jnp.bfloat16), row_max + jnp.log(totals))


def row_backward(entries):
    queries, key_rows, values, allowed, log_total, grad_mixture = entries
    masked = band_scores(queries, key_rows, allowed)
    attn_probs = jnp.where(allowed[None], jnp.exp(masked - log_total), 0.0)
    grad_probs = jnp.einsum(
        "qhd,khd->hqk", grad_mixture, values, preferred_element_type=jnp.float32
    )
    grad_values = jnp.einsum(
        "hqk,qhd->khd",
        attn_probs.astype(jnp.bfloat16),
        grad_mixture,
        preferred_element_type=jnp.float32,
    )
    inner = jnp.sum(grad_probs * attn_probs, -1, keepdims=True)
    grad_scores = (attn_probs * (grad_probs - inner)).astype(jnp.bfloat16)
    grad_queries = jnp.einsum(
        "hqk,khd->qhd", grad_scores, key_rows, preferred_element_type=jnp.float32
    ) * HDIM ** (-0.5)
    grad_keys = jnp.einsum(
        "hqk,qhd->khd", grad_scores, queries, preferred_element_type=jnp.float32
    ) * HDIM ** (-0.5)
    return (grad_queries, grad_keys, grad_values)


def unpack_edges(extended, row_count, extent, head_count):
    key_ext = extended[0][0].reshape(row_count, extent, head_count, HDIM)
    value_ext = extended[0][1].reshape(row_count, extent, head_count, HDIM)
    tag_ext = extended[1][0].astype(jnp.float32)
    return (key_ext, value_ext, tag_ext)


def body(
    tokens,
    segment_ids,
    padding_mask,
    qkv_weight,
    out_weight,
    wide_weight,
    narrow_weight,
    first_gain,
    second_gain,
    cotangent,
):
    row_count, seq_span, model_width = tokens.shape
    head_count = model_width // HDIM
    token_count = row_count * seq_span
    extent = seq_span + 2 * HALF
    gathered = (
        lax.all_gather(qkv_weight, ("batch", "seq"), axis=0, tiled=True),
        lax.all_gather(out_weight, ("batch", "seq"), axis=0, tiled=True),
        lax.all_gather(wide_weight, ("batch", "seq"), axis=0, tiled=True),
        lax.all_gather(narrow_weight, ("batch", "seq"), axis=0, tiled=True),
        lax.all_gather(first_gain, ("batch", "seq"), axis=0, tiled=True),
        lax.all_gather(second_gain, ("batch", "seq"), axis=0, tiled=True),
    )
    qkv_full, out_full, wide_full, narrow_full = (
        gathered[0],
        gathered[1],
        gathered[2],
        gathered[3],
    )
    gain_one = gathered[4].astype(jnp.float32)
    gain_two = gathered[5].astype(jnp.float32)
    hidden = tokens.reshape(token_count, model_width).astype(jnp.float32)
    normed, unit_one, inv_one = norm_forward(hidden, gain_one)
    normed_low = normed.astype(jnp.bfloat16)
    projected = jnp.dot(normed_low, qkv_full, preferred_element_type=jnp.float32)
    positions = (lax.axis_index("seq") * seq_span + jnp.arange(seq_span, dtype=jnp.int32)).astype(
        jnp.float32
    )
    angles = rope_angles(positions)
    shaped = projected.reshape(row_count, seq_span, 3, head_count, HDIM)
    queries = rotate(shaped[:, :, 0], angles).astype(jnp.bfloat16)
    key_rows = rotate(shaped[:, :, 1], angles).astype(jnp.bfloat16)
    values = shaped[:, :, 2].astype(jnp.bfloat16)
    key_tags = (
        jnp.where(padding_mask == 1, segment_ids + 1, 0).astype(jnp.float32).astype(jnp.bfloat16)
    )
    tag_rows = key_tags[None]
    packed = jnp.stack(
        [
            key_rows.reshape(row_count, seq_span, model_width),
            values.reshape(row_count, seq_span, model_width),
        ]
    )
    extended = (with_halo(packed, (("seq", 2),), HALF), with_halo(tag_rows, (("seq", 2),), HALF))
    key_ext, value_ext, tag_ext = unpack_edges(extended, row_count, extent, head_count)
    offsets = (
        jnp.arange(extent, dtype=jnp.int32)[None, :]
        - HALF
        - jnp.arange(seq_span, dtype=jnp.int32)[:, None]
    )
    in_band = jnp.abs(offsets) <= HALF
    query_tags = (segment_ids + 1).astype(jnp.float32)
    same_doc = tag_ext[:, None, :] == query_tags[:, :, None]
    allowed = in_band[None] & (same_doc | (offsets == 0)[None])
    mixture, log_total = lax.map(row_forward, (queries, key_ext, value_ext, allowed))
    attended = mixture.reshape(token_count, model_width)
    branch = jnp.dot(attended, out_full, preferred_element_type=jnp.float32)
    middle = hidden + branch
    second, unit_two, inv_two = norm_forward(middle, gain_two)
    second_low = second.astype(jnp.bfloat16)
    expanded = jnp.dot(second_low, wide_full, preferred_element_type=jnp.float32)
    gate_in = expanded[:, :FF]
    gate_up = expanded[:, FF:]
    activated = gated_unit(gate_in, gate_up).astype(jnp.bfloat16)
    result = middle + jnp.einsum(
        "nf,df->nd", activated, narrow_full, preferred_element_type=jnp.float32
    )
    outputs = result.astype(jnp.bfloat16).reshape(row_count, seq_span, model_width)
    cot_low = cotangent.reshape(token_count, model_width)
    grad_act = jnp.einsum("nd,df->nf", cot_low, narrow_full, preferred_element_type=jnp.float32)
    grad_narrow = jnp.einsum("nd,nf->df", cot_low, activated, preferred_element_type=jnp.float32)
    _, pullback = jax.vjp(gated_unit, gate_in, gate_up)
    grad_gate_in, grad_gate_up = pullback(grad_act)
    grad_expanded = jnp.concatenate([grad_gate_in, grad_gate_up], -1).astype(jnp.bfloat16)
    grad_wide = jnp.einsum(
        "nd,nf->df", second_low, grad_expanded, preferred_element_type=jnp.float32
    )
    grad_second = jnp.einsum(
        "nf,df->nd", grad_expanded, wide_full, preferred_element_type=jnp.float32
    )
    grad_mid_norm, grad_gain_two = norm_backward(grad_second, unit_two, inv_two, gain_two)
    grad_middle = cot_low.astype(jnp.float32) + grad_mid_norm
    grad_branch = grad_middle.astype(jnp.bfloat16)
    grad_out_weight = jnp.einsum(
        "nd,ne->de", attended, grad_branch, preferred_element_type=jnp.float32
    )
    grad_attended = jnp.einsum(
        "ne,de->nd", grad_branch, out_full, preferred_element_type=jnp.float32
    ).astype(jnp.bfloat16)
    grad_attended = grad_attended.reshape(row_count, seq_span, head_count, HDIM)
    grad_queries, grad_key_ext, grad_value_ext = lax.map(
        row_backward, (queries, key_ext, value_ext, allowed, log_total, grad_attended)
    )
    edge_stack = jnp.stack(
        [
            grad_key_ext.reshape(row_count, extent, model_width),
            grad_value_ext.reshape(row_count, extent, model_width),
        ]
    )
    outgoing = jnp.concatenate([edge_stack[:, :, :HALF], edge_stack[:, :, extent - HALF :]], axis=2)
    incoming = with_halo(outgoing.astype(jnp.bfloat16), (("seq", 2),), HALF).astype(outgoing.dtype)
    owned_grads = edge_stack[:, :, HALF : HALF + seq_span]
    owned_grads = jnp.concatenate(
        [
            owned_grads[:, :, :HALF] + incoming[:, :, :HALF],
            owned_grads[:, :, HALF : seq_span - HALF],
            owned_grads[:, :, seq_span - HALF :] + incoming[:, :, 3 * HALF :],
        ],
        axis=2,
    )
    grad_keys = owned_grads[0].reshape(row_count, seq_span, head_count, HDIM)
    grad_values = owned_grads[1].reshape(row_count, seq_span, head_count, HDIM)
    grad_q_pre = rotate(grad_queries, -angles)
    grad_k_pre = rotate(grad_keys, -angles)
    grad_projected = (
        jnp.stack([grad_q_pre, grad_k_pre, grad_values], axis=2)
        .reshape(token_count, 3 * model_width)
        .astype(jnp.bfloat16)
    )
    grad_qkv = jnp.einsum(
        "nd,ne->de", normed_low, grad_projected, preferred_element_type=jnp.float32
    )
    grad_normed = jnp.einsum(
        "ne,de->nd", grad_projected, qkv_full, preferred_element_type=jnp.float32
    )
    grad_in_norm, grad_gain_one = norm_backward(grad_normed, unit_one, inv_one, gain_one)
    grad_tokens = (
        (grad_middle + grad_in_norm).astype(jnp.bfloat16).reshape(row_count, seq_span, model_width)
    )
    joined = jnp.concatenate(
        [
            grad_qkv,
            grad_out_weight,
            grad_wide,
            grad_narrow,
            grad_gain_one[:, None],
            grad_gain_two[:, None],
        ],
        axis=1,
    )
    shards = lax.psum_scatter(joined, ("batch", "seq"), scatter_dimension=0, tiled=True)
    first_end = 3 * model_width
    second_end = first_end + model_width
    third_end = second_end + 2 * FF
    fourth_end = third_end + FF
    return (
        outputs,
        grad_tokens,
        shards[:, :first_end],
        shards[:, first_end:second_end],
        shards[:, second_end:third_end],
        shards[:, third_end:fourth_end],
        shards[:, fourth_end],
        shards[:, fourth_end + 1],
    )


def solution(mesh):
    placed = (
        P("batch", "seq", None),
        P("batch", "seq"),
        P("batch", "seq"),
        P(("batch", "seq"), None),
        P(("batch", "seq"), None),
        P(("batch", "seq"), None),
        P(("batch", "seq"), None),
        P(("batch", "seq")),
        P(("batch", "seq")),
        P("batch", "seq", None),
    )
    return jax.shard_map(
        body,
        mesh=mesh,
        in_specs=placed,
        out_specs=(
            P("batch", "seq", None),
            P("batch", "seq", None),
            P(("batch", "seq"), None),
            P(("batch", "seq"), None),
            P(("batch", "seq"), None),
            P(("batch", "seq"), None),
            P(("batch", "seq")),
            P(("batch", "seq")),
        ),
        check_vma=False,
    )
```

profile of v0, /device:TPU:0, one launch (start us, length us, event | category | flops | bytes accessed | tf_op | source)
XLA Modules:
  0.0 1568.0 jit_solution(4059918210831989545)
XLA Ops:
  10.2 4.9 collective-permute-start.2
  19.7 41.8 %all-reduce.2 = (bf16[1024]{0:T(1024)(128)(2,1)S(1)}, bf16[1024]{0:T(1024)(128)(2,1)S(1)}) all-reduce(bf16[1024]{0:T(1024)(128)(2,1)S(1)} %dynamic-update-slice, bf16[1024]{0:T(1024)(128)(2,1)S(1)} %dynamic-update-slice.1), channel_id=1, replica_groups=mesh['batch'=8,'seq'=4] {'batch','seq'}, use_global_device_ids=true, to_apply=%add | all-reduce | flops 2048 | bytes 8192
  64.5 18.7 %all-gather.5.cloned.1.call-done = bf16[1024,3072]{1,0:T(8,128)(2,1)} async-done(((bf16[32,3072]{1,0:T(8,128)(2,1)}), bf16[1024,3072]{1,0:T(8,128)(2,1)}) %all-gather.5.cloned.1.call-update) | async-done | bytes 6291472 | tf_op jit(solution)/shard_map/all_gather | solution.py:135
  83.2 8.6 copy.60
  91.8 6.3 fusion.75
  104.7 4.9 collective-permute-start
  112.6 9.7 collective-permute-done.1
  125.9 4.1 pad_maximum_fusion.5
  131.5 13.6 while.26
  149.0 3.5 fusion.96
  154.2 77.3 %all-gather.9.cloned.1.call-done = bf16[1024,5248]{1,0:T(8,128)(2,1)} async-done(((bf16[32,5248]{1,0:T(8,128)(2,1)}), bf16[1024,5248]{1,0:T(8,128)(2,1)}) %all-gather.9.cloned.1.call-update) | async-done | bytes 10747920 | tf_op jit(solution)/shard_map/all_gather | solution.py:137
  231.5 13.0 fusion.91
  244.5 54.4 %all-gather.11.cloned.1.call-done = bf16[1024,2624]{1,0:T(8,128)(2,1)} async-done(((bf16[32,2624]{1,0:T(8,128)(2,1)}), bf16[1024,2624]{1,0:T(8,128)(2,1)}) %all-gather.11.cloned.1.call-update) | async-done | bytes 5373968 | tf_op jit(solution)/shard_map/all_gather | solution.py:138
  298.8 20.7 %add_convert_fusion = (bf16[512,2624]{1,0:T(8,128)(2,1)}, f32[512,2624]{1,0:T(8,128)S(1)}, f32[512,2624]{1,0:T(8,128)}) fusion(f32[512,5248]{1,0:T(8,128)} %fusion.91, bf16[512,1024]{1,0:T(8,128)(2,1)S(1)} %bitcast.232, bf16[1024,2624]{1,0:T(8,128)(2,1)} %all-gather.11.cloned.1.call-done), kind=kOutput, calls=%fused_computation.68 | convolution fusion | flops 2849538048 | bytes 30605312 | tf_op jit(solution)/shard_map/nd,df->nf/dot_general | solution.py:198
  319.6 5.2 multiply_convert_fusion.1
  324.7 12.2 multiply_reduce_fusion.1
  344.5 2.9 copy.70
  347.4 26.7 %while.27 = (s32[]{:T(128)}, f32[2,256,16,64]{1,3,2,0:T(8,128)}, f32[2,384,16,64]{1,3,2,0:T(8,128)}, f32[2,384,16,64]{1,3,2,0:T(8,128)}, bf16[2,384,16,64]{1,3,2...) while((s32[]{:T(128)}, f32[2,256,16,64]{1,3,2,0:T(8,128)}, ...), condition=%wide.region_12.13_spmd, body=%wide.region_10.12_spmd.sunk | while | flops 1023012864 | bytes 133813608 | solution.py:219
  347.5 3.2 exponential_select_fusion.3
  360.8 3.2 exponential_select_fusion.3
  374.1 3.2 fusion.56
  381.4 3.4 fusion.77
  386.1 10.8 fusion.52
  405.6 5.5 collective-permute-start.4
  411.1 9.3 convolution_bitcast_fusion
  425.6 3.3 maximum_convert_fusion.1
  435.5 3.7 copy.75
  440.5 5.3 fusion.73
  446.9 10.3 fusion.97
  457.1 57.7 %concatenate.45 = f32[1024,11970]{1,0:T(8,128)} concatenate(f32[1024,3072]{1,0:T(8,128)} %fusion.97, f32[1024,1024]{1,0:T(8,128)} %fusion.77, f32[1024,5248]{1,0:T(8,128)} %fusion.52, f32[1024,2624]{1,0:T(8,128)} %convolution_bitcast_fusion, f32[1024,1]{1,0:T(8,128)} %copy.78, f32[1024,1]{1,0:T(8,128)} %copy.79), dimensions={1} | concatenate | bytes 98058240 | tf_op jit(solution)/shard_map/concatenate | solution.py:258
  514.9 7.7 add_convert_fusion.1
  524.3 1028.4 %reduce-scatter.2.cloned.1.call-done = f32[32,11970]{1,0:T(8,128)} async-done(((f32[1024,11970]{1,0:T(8,128)}), f32[32,11970]{1,0:T(8,128)}) %reduce-scatter.2.cloned.1.call-update) | async-done | bytes 1532176 | tf_op jit(solution)/shard_map/reduce_scatter | solution.py:269
  (231 shorter events, 110.0 us)
Async XLA Ops:
  7.2 57.0 %copy-start.13 = (bf16[2,256,1024]{2,1,0:T(8,128)(2,1)S(1)}, bf16[2,256,1024]{2,1,0:T(8,128)(2,1)}, u32[]{:S(2)}) copy-start(bf16[2,256,1024]{2,1,0:T(8,128)(2,1)} %param.14) | copy-start | bytes 3145732
  7.2 76.0 %all-gather.5.cloned.1.call-start = ((), (), s32[]{:S(2)}) async-start(), calls=%async_computation.1 | async-start | bytes 6488064 | tf_op jit(solution)/shard_map/all_gather | solution.py:135
  7.9 141.0 %all-gather.7.cloned.1.call-start = ((), (), s32[]{:S(2)}) async-start(), calls=%async_computation.2 | async-start | bytes 2162688 | tf_op jit(solution)/shard_map/all_gather | solution.py:136
  8.7 222.8 %all-gather.9.cloned.1.call-start = ((), (), s32[]{:S(2)}) async-start(), calls=%async_computation.3 | async-start | bytes 11083776 | tf_op jit(solution)/shard_map/all_gather | solution.py:137
  9.4 289.4 %all-gather.11.cloned.1.call-start = ((), (), s32[]{:S(2)}) async-start(), calls=%async_computation.4 | async-start | bytes 5677056 | tf_op jit(solution)/shard_map/all_gather | solution.py:138
  10.2 100.8 %collective-permute-start.2 = (bf16[1,2,64]{2,1,0:T(2,128)(2,1)S(1)}, bf16[1,2,64]{2,1,0:T(2,128)(2,1)S(1)}, u32[]{:S(2)}, u32[]{:S(2)}) collective-permute-start(bf16[1,2,64]{2,1,0:T(2,128)(2,1)S(1)} %get-tuple-element.238), channel_id=1, source_target_pairs={{0,1},{1,2},{2,3},{4,5},{5,6},{6,7},{8,9},{9,10},{10,11},{12,13},{... | collective-permute-start | bytes 776 | tf_op jit(solution)/shard_map/ppermute | solution.py:23
  15.1 95.8 %collective-permute-start.3 = (bf16[1,2,64]{2,1,0:T(2,128)(2,1)S(1)}, bf16[1,2,64]{2,1,0:T(2,128)(2,1)S(1)}, u32[]{:S(2)}, u32[]{:S(2)}) collective-permute-start(bf16[1,2,64]{2,1,0:T(2,128)(2,1)S(1)} %get-tuple-element.239), channel_id=1, source_target_pairs={{1,0},{2,1},{3,2},{5,4},{6,5},{7,6},{9,8},{10,9},{11,10},{13,12},{... | collective-permute-start | bytes 776 | tf_op jit(solution)/shard_map/ppermute | solution.py:24
  16.5 1536.2 %reduce-scatter.2.cloned.1.call-start = ((), (), s32[]{:S(2)}) async-start(), calls=%async_computation.5 | async-start | bytes 50823168 | tf_op jit(solution)/shard_map/reduce_scatter | solution.py:269
  64.5 27.3 %copy-start.31 = (bf16[2,256,1024]{2,1,0:T(8,128)(2,1)}, bf16[2,256,1024]{2,1,0:T(8,128)(2,1)S(1)}, u32[]{:S(2)}) copy-start(bf16[2,256,1024]{2,1,0:T(8,128)(2,1)S(1)} %fusion.63) | copy-start | bytes 3145732
  103.4 18.9 %collective-permute-start.1 = (bf16[2,2,64,1024]{3,2,1,0:T(8,128)(2,1)S(1)}, bf16[2,2,64,1024]{3,2,1,0:T(8,128)(2,1)}, u32[]{:S(2)}, u32[]{:S(2)}) collective-permute-start(bf16[2,2,64,1024]{3,2,1,0:T(8,128)(2,1)S(1)} %copy.63), channel_id=1, source_target_pairs={{1,0},{2,1},{3,2},{5,4},{6,5},{7,6},{9,8},{10,9},{11,10},{13,12},{... | collective-permute-start | bytes 1572872 | tf_op jit(solution)/shard_map/ppermute | solution.py:24
  104.7 19.9 %collective-permute-start = (bf16[2,2,64,1024]{3,2,1,0:T(8,128)(2,1)}, bf16[2,2,64,1024]{3,2,1,0:T(8,128)(2,1)S(1)}, u32[]{:S(2)}, u32[]{:S(2)}) collective-permute-start(bf16[2,2,64,1024]{3,2,1,0:T(8,128)(2,1)} %copy.62), channel_id=1, source_target_pairs={{0,1},{1,2},{2,3},{4,5},{5,6},{6,7},{8,9},{9,10},{10,11},{12,13},{... | collective-permute-start | bytes 1572872 | tf_op jit(solution)/shard_map/ppermute | solution.py:23
  145.1 7.4 copy-start
  154.2 144.6 %copy-start.34 = (bf16[2,256,1024]{2,1,0:T(8,128)(2,1)S(1)}, bf16[2,256,1024]{2,1,0:T(8,128)(2,1)}, u32[]{:S(2)}) copy-start(bf16[2,256,1024]{2,1,0:T(8,128)(2,1)} %param.23) | copy-start | bytes 3145732
  298.8 20.7 %slice-start = ((s8[10747904]{0:T(1024)(128)(4,1)}), s8[4194304]{0:T(1024)(128)(4,1)S(1)}, s32[]{:S(2)}) async-start(s8[10747904]{0:T(1024)(128)(4,1)} %bitcast.215), calls=%async_computation.6 | async-start | bytes 8388608
  298.8 20.7 %slice-start.1 = ((s8[10747904]{0:T(1024)(128)(4,1)}), s8[4194304]{0:T(1024)(128)(4,1)S(1)}, s32[]{:S(2)}) async-start(s8[10747904]{0:T(1024)(128)(4,1)} %bitcast.215), calls=%async_computation.7 | async-start | bytes 8388608
  298.8 20.7 %slice-start.2 = ((s8[10747904]{0:T(1024)(128)(4,1)}), s8[2359296]{0:T(1024)(128)(4,1)S(1)}, s32[]{:S(2)}) async-start(s8[10747904]{0:T(1024)(128)(4,1)} %bitcast.215), calls=%async_computation.8 | async-start | bytes 4718592
  319.5 5.2 copy-start.3
  336.9 3.9 copy-start.29
  347.5 3.2 copy-start.5
  374.1 4.3 copy-start.11
  381.4 3.4 copy-start.4
  381.4 3.4 copy-start.21
  381.4 4.8 copy-start.25
  404.3 16.6 %collective-permute-start.5 = (bf16[2,2,64,1024]{3,2,1,0:T(8,128)(2,1)}, bf16[2,2,64,1024]{3,2,1,0:T(8,128)(2,1)}, u32[]{:S(2)}, u32[]{:S(2)}) collective-permute-start(bf16[2,2,64,1024]{3,2,1,0:T(8,128)(2,1)} %copy.72), channel_id=1, source_target_pairs={{1,0},{2,1},{3,2},{5,4},{6,5},{7,6},{9,8},{10,9},{11,10},{13,12},{... | collective-permute-start | bytes 1572872 | tf_op jit(solution)/shard_map/ppermute | solution.py:24
  405.6 17.6 %collective-permute-start.4 = (bf16[2,2,64,1024]{3,2,1,0:T(8,128)(2,1)}, bf16[2,2,64,1024]{3,2,1,0:T(8,128)(2,1)}, u32[]{:S(2)}, u32[]{:S(2)}) collective-permute-start(bf16[2,2,64,1024]{3,2,1,0:T(8,128)(2,1)} %copy.71), channel_id=1, source_target_pairs={{0,1},{1,2},{2,3},{4,5},{5,6},{6,7},{8,9},{9,10},{10,11},{12,13},{... | collective-permute-start | bytes 1572872 | tf_op jit(solution)/shard_map/ppermute | solution.py:23
  425.6 3.3 copy-start.8
  425.6 3.8 copy-start.12
  435.2 4.9 slice-start.3
  435.5 4.5 slice-start.4
  440.0 5.8 copy-start.24
  514.9 7.7 copy-start.19
  514.9 7.7 copy-start.30
  (36 other events, 61.5 us)
Sparse Core Ops, SparseCore 0:
  10.9 72.2 all-gather.4
  86.1 55.6 all-gather.6
  144.7 86.7 all-gather.8
  234.1 64.6 all-gather.10
  515.0 1037.6 reduce-scatter.1
where the time goes:
time: 1580 us; the launch traced here: 1570 us
  waiting for transfers between devices  1190 us (75%)
  local copies, waits for them, and re-layouts  135 us (9%)
  matrix products  125 us (8%)
  blocking collectives  41.8 us (3%)
  other arithmetic  41.1 us (3%)
  starting transfers between devices  19.4 us (1%)
    reduce_scatter x1, waiting for transfers between devices, body(): lax.psum_scatter(joined, ('batch', 'seq'), scatter_dimension=0, tiled=True)  1030 us
    all_gather x1, waiting for transfers between devices, body(): lax.all_gather(wide_weight, ('batch', 'seq'), axis=0, tiled=True)  77.3 us
    concatenate x1, local copies, waits for them, and re-layouts, body(): jnp.concatenate([grad_qkv, grad_out_weight, grad_wide, grad_narrow, grad_...  57.7 us
    all_gather x1, waiting for transfers between devices, body(): lax.all_gather(narrow_weight, ('batch', 'seq'), axis=0, tiled=True)  54.4 us
    unnamed x1, blocking collectives  41.8 us
  transfers between devices with their start and end apart: 11, of which 6 were waited for; matrix products, arithmetic and copies ran while one was open for 6% of the time, Pallas kernels for 0%

commit v1 on v0

--- a/solution.py
+++ b/solution.py
@@ -1,16 +1,404 @@
+import functools
+
 import jax
 import jax.numpy as jnp
 from jax import lax
+from jax.experimental import pallas as pl
+from jax.experimental.pallas import tpu as pltpu
 from jax.sharding import PartitionSpec as P
 
+MESH = pl.DeviceIdType.MESH
 HDIM = 64
 FF = 2624
+PADDED = 2688
 HALF = 64
-
-
 NORM_EPS = 1e-05
 MASK_FILL = -1e30
 ROPE_BASE = 10000.0
+
+
+GATHER_STREAMS = (
+    ("zxy", "g", 0, 128),
+    ("zxy", "q", 0, 768),
+    ("zyx", "q", 768, 640),
+    ("yxz", "q", 1408, 128),
+    ("zxy", "q", 1536, 640),
+    ("zyx", "q", 2176, 640),
+    ("xyz", "q", 2816, 128),
+    ("yxz", "q", 2944, 128),
+    ("zxy", "o", 0, 384),
+    ("zyx", "o", 384, 384),
+    ("yxz", "o", 768, 256),
+    ("zxy", "w", 0, 640),
+    ("zyx", "w", 640, 640),
+    ("xyz", "w", 1280, 384),
+    ("yxz", "w", 1664, 128),
+    ("zxy", "w", 1792, 640),
+    ("zyx", "w", 2432, 640),
+    ("xyz", "w", 3072, 384),
+    ("yxz", "w", 3456, 128),
+    ("zxy", "w", 3584, 768),
+    ("zyx", "w", 4352, 768),
+    ("xyz", "w", 5120, 128),
+    ("yxz", "w", 5248, 128),
+    ("zxy", "n", 0, 640),
+    ("zyx", "n", 640, 512),
+    ("xyz", "n", 1152, 256),
+    ("yxz", "n", 1408, 384),
+    ("zxy", "n", 1792, 256),
+    ("zyx", "n", 2048, 128),
+    ("yxz", "n", 2176, 512),
+)
+GATHER_ORDER = (
+    0, 7, 14, 21, 28, 42, 49, 70, 91, 98, 1, 119, 35, 22, 126, 43, 50, 147, 154, 8, 71, 99, 175, 92,
+    182, 15, 127, 2, 120, 23, 155, 203, 29, 44, 9, 3, 51, 56, 16, 63, 24, 4, 10, 17, 25, 72, 5, 36,
+    77, 30, 6, 84, 26, 37, 45, 27, 18, 52, 11, 100, 93, 46, 31, 53, 47, 54, 38, 57, 105, 48, 64, 58,
+    55, 65, 19, 73, 112, 59, 128, 12, 74, 20, 32, 121, 75, 78, 13, 85, 39, 76, 133, 79, 86, 66, 101,
+    140, 60, 94, 80, 156, 102, 33, 161, 87, 40, 95, 168, 67, 103, 34, 189, 196, 41, 104, 96, 81,
+    106, 61, 113, 97, 107, 114, 62, 129, 68, 88, 122, 69, 115, 108, 130, 123, 131, 82, 132, 89, 148,
+    124, 134, 83, 183, 116, 141, 90, 135, 109, 125, 142, 157, 149, 136, 143, 150, 184, 158, 159,
+    151, 117, 162, 160, 169, 110, 152, 176, 163, 118, 170, 204, 164, 137, 111, 153, 144, 185, 177,
+    171, 186, 205, 187, 165, 178, 190, 188, 138, 197, 191, 198, 192, 179, 172, 139, 145, 206, 199,
+    193, 180, 146, 181, 207, 166, 173, 200, 208, 167, 201, 194, 174, 209, 202, 195,
+)
+SCATTER_STREAMS = (
+    ("zxy", "n", 1792, 384),
+    ("zyx", "n", 2176, 384),
+    ("yxz", "n", 2560, 128),
+    ("zxy", "n", 0, 768),
+    ("zyx", "n", 768, 640),
+    ("xyz", "n", 1408, 128),
+    ("yxz", "n", 1536, 256),
+    ("zxy", "w", 3584, 640),
+    ("zyx", "w", 4224, 640),
+    ("xyz", "w", 4864, 256),
+    ("yxz", "w", 5120, 256),
+    ("zxy", "w", 1792, 640),
+    ("zyx", "w", 2432, 640),
+    ("xyz", "w", 3072, 384),
+    ("yxz", "w", 3456, 128),
+    ("zxy", "w", 0, 640),
+    ("zyx", "w", 640, 640),
+    ("xyz", "w", 1280, 128),
+    ("yxz", "w", 1408, 384),
+    ("zxy", "o", 0, 512),
+    ("zyx", "o", 512, 256),
+    ("xyz", "o", 768, 256),
+    ("zxy", "q", 1536, 640),
+    ("zyx", "q", 2176, 512),
+    ("xyz", "q", 2688, 384),
+    ("zxy", "q", 0, 640),
+    ("zyx", "q", 640, 768),
+    ("xyz", "q", 1408, 128),
+    ("yxz", "g", 0, 128),
+)
+SCATTER_ORDER = (
+    0, 7, 14, 21, 1, 28, 8, 15, 35, 42, 49, 22, 16, 56, 29, 36, 43, 17, 63, 70, 77, 37, 84, 44, 38,
+    91, 64, 98, 2, 105, 45, 71, 9, 112, 18, 30, 65, 119, 23, 126, 133, 72, 3, 10, 140, 147, 19, 39,
+    46, 154, 50, 57, 4, 66, 161, 11, 20, 31, 168, 24, 175, 5, 12, 182, 32, 6, 13, 25, 189, 47, 196,
+    67, 40, 33, 78, 73, 85, 92, 26, 48, 41, 34, 99, 27, 93, 58, 100, 51, 94, 120, 74, 127, 101, 86,
+    68, 79, 59, 52, 69, 75, 95, 102, 113, 106, 60, 76, 53, 87, 80, 61, 54, 88, 62, 81, 96, 103, 134,
+    55, 141, 121, 89, 128, 82, 104, 97, 107, 90, 122, 83, 114, 129, 148, 162, 108, 123, 142, 149,
+    155, 115, 130, 109, 124, 135, 116, 150, 110, 125, 143, 183, 169, 117, 111, 131, 151, 144, 136,
+    163, 118, 145, 132, 170, 176, 146, 137, 152, 156, 164, 171, 138, 153, 190, 165, 172, 197, 139,
+    184, 191, 166, 157, 177, 192, 198, 167, 158, 173, 193, 199, 159, 178, 185, 174, 194, 200, 179,
+    160, 195, 201, 186, 180, 202, 187, 181, 188,
+)
+
+
+def place():
+    b=lax.axis_index("batch"); z=lax.axis_index("seq")
+    return b, z, b//4, (b//2)%2, b%2
+
+def enter(zn):
+    bar=pltpu.get_barrier_semaphore()
+    b,z,_,_,_=place()
+    for m in (1,2,4):
+        pl.semaphore_signal(bar,1,device_id=(b^m,z),device_id_type=MESH)
+    @pl.when(z<zn-1)
+    def _(): pl.semaphore_signal(bar,1,device_id=(b,z+1),device_id_type=MESH)
+    @pl.when(z>0)
+    def _(): pl.semaphore_signal(bar,1,device_id=(b,z-1),device_id_type=MESH)
+    pl.semaphore_wait(bar,3+(z<zn-1).astype(jnp.int32)+(z>0).astype(jnp.int32))
+
+class Counter:
+    def __init__(self): self.n=0
+    def take(self,k=1):
+        r=self.n; self.n+=k; return r
+
+def gather_steps(streams, shards, fulls, ssem, rsem, ctr):
+    b,z,y,x,c=place()
+    out=[]; finals=[]
+    def rdma(src,dst,i,dev):
+        return pltpu.make_async_remote_copy(src,dst,ssem.at[i],rsem.at[i],device_id=dev,device_id_type=MESH)
+    for (order,name,c0,cn) in streams:
+        full=fulls[name]; cols=pl.ds(c0,cn)
+        region={}
+        def idx(region, zz=None, flip=None):
+            yy=slice(None) if 'y' in region else ((1-y) if flip=='y' else y)
+            xx=slice(None) if 'x' in region else ((1-x) if flip=='x' else x)
+            if zz is None: zi=slice(None) if 'z' in region else pl.ds(pl.multiple_of(z*32,32),32)
+            else: zi=pl.ds(pl.multiple_of(zz*32,32),32)
+            return full.at[yy,xx,c,zi,cols]
+        steps=[]; pending=None; first=True
+        for d in order:
+            own=shards[name].at[:,cols] if not region else None
+            if d in 'xy':
+                i=ctr.take(); dev=(b^(2 if d=='x' else 4), z)
+                cp=rdma(idx(region) if own is None else own, idx(region), i, dev)
+                rc=rdma(idx(region,flip=d),idx(region,flip=d),i,dev)
+                def fn(pending=pending,cp=cp):
+                    if pending: pending()
+                    cp.start()
+                steps.append(fn); pending=rc.wait_recv
+                finals.append(cp.wait_send)
+                region=dict(region); region[d]=True
+            else:
+                for hop in range(3):
+                    i=ctr.take(2)
+                    cu=jnp.logical_and(z-hop>=0, z<3); cd=jnp.logical_and(z+hop<=3, z>0)
+                    pu=jnp.maximum(z-hop,0); pd=jnp.minimum(z+hop,3)
+                    o=own if hop==0 else None
+                    up=rdma(o if o is not None else idx(region,pu), idx(region,pu), i, (b,jnp.minimum(z+1,3)))
+                    dn=rdma(o if o is not None else idx(region,pd), idx(region,pd), i+1, (b,jnp.maximum(z-1,0)))
+                    ru=z-1-hop>=0; rd=z+1+hop<=3
+                    rpu=jnp.maximum(z-1-hop,0); rpd=jnp.minimum(z+1+hop,3)
+                    wu=rdma(idx(region,rpu),idx(region,rpu),i,(b,jnp.minimum(z+1,3)))
+                    wd=rdma(idx(region,rpd),idx(region,rpd),i+1,(b,jnp.maximum(z-1,0)))
+                    def fn(pending=pending,up=up,dn=dn,cu=cu,cd=cd):
+                        if pending: pending()
+                        pl.when(cu)(up.start); pl.when(cd)(dn.start)
+                    steps.append(fn)
+                    def pending(wu=wu,wd=wd,ru=ru,rd=rd):
+                        pl.when(ru)(wu.wait_recv); pl.when(rd)(wd.wait_recv)
+                    def fin(up=up,dn=dn,cu=cu,cd=cd):
+                        pl.when(cu)(up.wait_send); pl.when(cd)(dn.wait_send)
+                    finals.append(fin)
+                region=dict(region); region['z']=True
+        i=ctr.take(); dev=(b^1,z)
+        cp=rdma(full.at[:,:,c,:,cols],full.at[:,:,c,:,cols],i,dev)
+        rc=rdma(full.at[:,:,1-c,:,cols],full.at[:,:,1-c,:,cols],i,dev)
+        def fn(pending=pending,cp=cp):
+            pending(); cp.start()
+        steps.append(fn)
+        steps.append(rc.wait_recv)
+        finals.append(cp.wait_send)
+        out.append(steps)
+    return out, finals
+
+def add_into(dst, a, b, rows, width):
+    def body(r):
+        s=pl.ds(pl.multiple_of(r*16,16),16)
+        dst[s,:]=a[s,:]+b[s,:]
+    if rows<=32:
+        for r in range(rows//16): body(r)
+    else:
+        pl.loop(0,rows//16)(body)
+
+def scatter_steps(streams, grads, acc, bufs, outs, ssem, rsem, ctr):
+    b,z,y,x,c=place()
+    out=[]; finals=[]
+    def rdma(src,dst,i,dev):
+        return pltpu.make_async_remote_copy(src,dst,ssem.at[i],rsem.at[i],device_id=dev,device_id_type=MESH)
+    def one(j,order,name,c0,cn):
+        G=grads[name]; A=acc[name]; cols=pl.ds(c0,cn); B=bufs[j]; O=outs[name]
+        steps=[]
+        i=ctr.take(); dev=(b^1,z)
+        cp=rdma(G.at[:,:,1-c,:,cols],B['c'],i,dev)
+        steps.append(cp.start); finals.append(cp.wait_send)
+        def pending(cp=cp):
+            cp.wait_recv()
+            for yy in range(2):
+                for xx in range(2):
+                    add_into(A.at[yy,xx,:,cols],A.at[yy,xx,:,cols],B['c'].at[yy,xx],128,cn)
+        whole={'x','y','z'}
+        def idx(fix, zz=None):
+            return A.at[fix.get('y',slice(None)),fix.get('x',slice(None)),(pl.ds(pl.multiple_of(zz*32,32),32) if zz is not None else fix.get('z',slice(None))),cols]
+        fix={}
+        rev=order[::-1]
+        for n,d in enumerate(rev):
+            last=n==2
+            if d in 'xy':
+                i=ctr.take(); mine=y if d=='y' else x
+                dev=(b^(2 if d=='x' else 4), z)
+                f_other=dict(fix); f_other[d]=1-mine
+                f_own=dict(fix); f_own[d]=mine
+                cp=rdma(idx(f_other),B[d],i,dev)
+                def fn(pending=pending,cp=cp):
+                    pending(); cp.start()
+                steps.append(fn); finals.append(cp.wait_send)
+                def pending(cp=cp,f_own=f_own,d=d,last=last):
+                    cp.wait_recv()
+                    dst=idx(f_own)
+                    if last:
+                        O[:,cols]=dst[...].astype(jnp.float32)+B[d][...].astype(jnp.float32)
+                    elif len(dst.shape)==2: add_into(dst,dst,B[d],dst.shape[0],cn)
+                    else:
+                        for q in range(2): add_into(dst.at[q],dst.at[q],B[d].at[q],dst.shape[1],cn)
+                fix=f_own
+            else:
+                lead=[q for q in 'yx' if q not in fix]
+                def acc_add(t,buf,fix=fix,lead=lead):
+                    dst=idx(fix,t); s=pl.ds(pl.multiple_of(t*32,32),32)
+                    if not lead: add_into(dst,dst,buf.at[s],32,cn)
+                    elif len(lead)==2:
+                        for yy in range(2):
+                            for xx in range(2): add_into(dst.at[yy,xx],dst.at[yy,xx],buf.at[yy,xx,s],32,cn)
+                    else:
+                        for q in range(2): add_into(dst.at[q],dst.at[q],buf.at[q,s],32,cn)
+                def bat(buf,t,lead=lead):
+                    return buf.at[tuple([slice(None)]*len(lead))+(pl.ds(pl.multiple_of(t*32,32),32),)]
+                prev=None
+                for h in (2,1,0):
+                    i=ctr.take(2)
+                    td=jnp.maximum(z-1-h,0); tu=jnp.minimum(z+1+h,3)
+                    cd=z-1-h>=0; cu=z+1+h<=3
+                    dn=rdma(idx(fix,td),bat(B['d'],td),i,(b,jnp.maximum(z-1,0)))
+                    up=rdma(idx(fix,tu),bat(B['u'],tu),i+1,(b,jnp.minimum(z+1,3)))
+                    rd=jnp.logical_and(z<3, z-h>=0); ru=jnp.logical_and(z>0, z+h<=3)
+                    rtd=jnp.maximum(z-h,0); rtu=jnp.minimum(z+h,3)
+                    wd=rdma(idx(fix,rtd),bat(B['d'],rtd),i,(b,jnp.maximum(z-1,0)))
+                    wu=rdma(idx(fix,rtu),bat(B['u'],rtu),i+1,(b,jnp.minimum(z+1,3)))
+                    def fn(pending=pending,up=up,dn=dn,cu=cu,cd=cd):
+                        pending()
+                        pl.when(cd)(dn.start); pl.when(cu)(up.start)
+                    steps.append(fn)
+                    def fin(up=up,dn=dn,cu=cu,cd=cd):
+                        pl.when(cd)(dn.wait_send); pl.when(cu)(up.wait_send)
+                    finals.append(fin)
+                    def pending(wd=wd,wu=wu,rd=rd,ru=ru,rtd=rtd,rtu=rtu,acc_add=acc_add):
+                        @pl.when(rd)
+                        def _():
+                            wd.wait_recv(); acc_add(rtd,B['d'])
+                        @pl.when(ru)
+                        def _():
+                            wu.wait_recv(); acc_add(rtu,B['u'])
+                fix=dict(fix); fix['z']=pl.ds(pl.multiple_of(z*32,32),32)
+                if last:
+                    def pending(pending=pending,fix=fix):
+                        pending()
+                        O[:,cols]=idx(fix)[...].astype(jnp.float32)
+        steps.append(pending)
+        out.append(steps)
+    for j,s in enumerate(streams): one(j,*s)
+    return out, finals
+
+def landing(streams):
+    res=[]
+    for (order,name,c0,cn) in streams:
+        d={'c':(2,2,128,cn)}
+        have={'x':2,'y':2}; zr=128
+        for q in order[::-1]:
+            if q in 'xy':
+                del have[q]
+                d[q]=tuple(have.values())+(zr,cn)
+            else:
+                d['d']=tuple(have.values())+(128,cn); d['u']=d['d']; zr=32
+        res.append(d)
+    return res
+
+
+WIDTHS = {"q": 3072, "g": 128, "o": 1024, "w": 2 * PADDED, "n": PADDED}
+NAMES = tuple(WIDTHS)
+
+
+def gather_kernel(*refs):
+    count = len(NAMES)
+    shards = dict(zip(NAMES, refs[:count]))
+    fulls = dict(zip(NAMES, refs[count : 2 * count]))
+    ssem, rsem, lsem = refs[2 * count :]
+    b, z, y, x, c = place()
+    local = [
+        pltpu.make_async_copy(
+            shards[n], fulls[n].at[y, x, c, pl.ds(pl.multiple_of(z * 32, 32), 32), :], lsem.at[i]
+        )
+        for i, n in enumerate(NAMES)
+    ]
+    for copy in local:
+        copy.start()
+    enter(4)
+    steps, finals = gather_steps(GATHER_STREAMS, shards, fulls, ssem, rsem, Counter())
+    flat = [f for s in steps for f in s]
+    for copy in local:
+        copy.wait()
+    for i in GATHER_ORDER:
+        flat[i]()
+    for f in finals:
+        f()
+
+
+def gather_weights(*shards):
+    fulls = pl.pallas_call(
+        gather_kernel,
+        out_shape=tuple(jax.ShapeDtypeStruct((2, 2, 2, 128, WIDTHS[n]), jnp.bfloat16) for n in NAMES),
+        in_specs=[pl.BlockSpec(memory_space=pltpu.VMEM)] * len(NAMES),
+        out_specs=tuple(pl.BlockSpec(memory_space=pl.ANY) for _ in NAMES),
+        scratch_shapes=[
+            pltpu.SemaphoreType.DMA((400,)),
+            pltpu.SemaphoreType.DMA((400,)),
+            pltpu.SemaphoreType.DMA((8,)),
+        ],
+        compiler_params=pltpu.CompilerParams(
+            collective_id=1, has_side_effects=True, vmem_limit_bytes=32 << 20
+        ),
+    )(*shards)
+    return [f.reshape(1024, f.shape[-1]) for f in fulls]
+
+
+def scatter_kernel(shapes, *refs):
+    count = len(NAMES)
+    grads = dict(zip(NAMES, refs[:count]))
+    outs = dict(zip(NAMES, refs[count : 2 * count]))
+    acc = dict(zip(NAMES, refs[2 * count : 3 * count]))
+    rest = list(refs[3 * count :])
+    bufs = []
+    for s in shapes:
+        bufs.append(dict(zip(s, rest[: len(s)])))
+        rest = rest[len(s) :]
+    ssem, rsem, lsem = rest
+    b, z, y, x, c = place()
+    local = [
+        pltpu.make_async_copy(grads[n].at[:, :, c], acc[n], lsem.at[i]) for i, n in enumerate(NAMES)
+    ]
+    for copy in local:
+        copy.start()
+    enter(4)
+    steps, finals = scatter_steps(SCATTER_STREAMS, grads, acc, bufs, outs, ssem, rsem, Counter())
+    flat = [f for s in steps for f in s]
+    for copy in local:
+        copy.wait()
+    for i in SCATTER_ORDER:
+        flat[i]()
+    for f in finals:
+        f()
+
+
+def scatter_grads(*grads):
+    shapes = landing(SCATTER_STREAMS)
+    grads = [g.reshape(2, 2, 2, 128, g.shape[-1]) for g in grads]
+    return pl.pallas_call(
+        functools.partial(scatter_kernel, shapes),
+        out_shape=tuple(jax.ShapeDtypeStruct((32, WIDTHS[n]), jnp.float32) for n in NAMES),
+        in_specs=[pl.BlockSpec(memory_space=pl.ANY)] * len(NAMES),
+        out_specs=tuple(pl.BlockSpec(memory_space=pltpu.VMEM) for n in NAMES),
+        scratch_shapes=[pltpu.VMEM((2, 2, 128, WIDTHS[n]), jnp.bfloat16) for n in NAMES]
+        + [pltpu.VMEM(v, jnp.bfloat16) for s in shapes for v in s.values()]
+        + [
+            pltpu.SemaphoreType.DMA((500,)),
+            pltpu.SemaphoreType.DMA((500,)),
+            pltpu.SemaphoreType.DMA((8,)),
+        ],
+        compiler_params=pltpu.CompilerParams(
+            collective_id=2, has_side_effects=True, vmem_limit_bytes=60 << 20
+        ),
+    )(*grads)
+
+
+def pad_halves(array):
+    lead = array.shape[:-1]
+    array = array.reshape(lead + (2, FF))
+    array = jnp.pad(array, [(0, 0)] * len(lead) + [(0, 0), (0, PADDED - FF)])
+    return array.reshape(lead + (2 * PADDED,))
 
 
 def with_halo(array, sides, width):
@@ -131,22 +519,22 @@
     head_count = model_width // HDIM
     token_count = row_count * seq_span
     extent = seq_span + 2 * HALF
-    gathered = (
-        lax.all_gather(qkv_weight, ("batch", "seq"), axis=0, tiled=True),
-        lax.all_gather(out_weight, ("batch", "seq"), axis=0, tiled=True),
-        lax.all_gather(wide_weight, ("batch", "seq"), axis=0, tiled=True),
-        lax.all_gather(narrow_weight, ("batch", "seq"), axis=0, tiled=True),
-        lax.all_gather(first_gain, ("batch", "seq"), axis=0, tiled=True),
-        lax.all_gather(second_gain, ("batch", "seq"), axis=0, tiled=True),
-    )
-    qkv_full, out_full, wide_full, narrow_full = (
-        gathered[0],
-        gathered[1],
-        gathered[2],
-        gathered[3],
-    )
-    gain_one = gathered[4].astype(jnp.float32)
-    gain_two = gathered[5].astype(jnp.float32)
+    direct = (lax.axis_size("batch"), lax.axis_size("seq")) == (8, 4)
+    gains = jnp.stack([first_gain, second_gain], axis=1)
+    shards = (
+        qkv_weight,
+        jnp.pad(gains, ((0, 0), (0, 126))),
+        out_weight,
+        pad_halves(wide_weight),
+        jnp.pad(narrow_weight, ((0, 0), (0, PADDED - FF))),
+    )
+    if direct:
+        gathered = gather_weights(*shards)
+    else:
+        gathered = [lax.all_gather(s, ("batch", "seq"), axis=0, tiled=True) for s in shards]
+    qkv_full, gains_full, out_full, wide_full, narrow_full = gathered
+    gain_one = gains_full[:, 0].astype(jnp.float32)
+    gain_two = gains_full[:, 1].astype(jnp.float32)
     hidden = tokens.reshape(token_count, model_width).astype(jnp.float32)
     normed, unit_one, inv_one = norm_forward(hidden, gain_one)
     normed_low = normed.astype(jnp.bfloat16)
@@ -187,8 +575,8 @@
     second, unit_two, inv_two = norm_forward(middle, gain_two)
     second_low = second.astype(jnp.bfloat16)
     expanded = jnp.dot(second_low, wide_full, preferred_element_type=jnp.float32)
-    gate_in = expanded[:, :FF]
-    gate_up = expanded[:, FF:]
+    gate_in = expanded[:, :PADDED]
+    gate_up = expanded[:, PADDED:]
     activated = gated_unit(gate_in, gate_up).astype(jnp.bfloat16)
     result = middle + jnp.einsum(
         "nf,df->nd", activated, narrow_full, preferred_element_type=jnp.float32
@@ -255,31 +643,28 @@
     grad_tokens = (
         (grad_middle + grad_in_norm).astype(jnp.bfloat16).reshape(row_count, seq_span, model_width)
     )
-    joined = jnp.concatenate(
-        [
-            grad_qkv,
-            grad_out_weight,
-            grad_wide,
-            grad_narrow,
-            grad_gain_one[:, None],
-            grad_gain_two[:, None],
-        ],
-        axis=1,
-    )
-    shards = lax.psum_scatter(joined, ("batch", "seq"), scatter_dimension=0, tiled=True)
-    first_end = 3 * model_width
-    second_end = first_end + model_width
-    third_end = second_end + 2 * FF
-    fourth_end = third_end + FF
+    grad_gains = jnp.pad(jnp.stack([grad_gain_one, grad_gain_two], axis=1), ((0, 0), (0, 126)))
+    grads = [
+        g.astype(jnp.bfloat16)
+        for g in (grad_qkv, grad_gains, grad_out_weight, grad_wide, grad_narrow)
+    ]
+    if direct:
+        sums = scatter_grads(*grads)
+    else:
+        sums = [
+            lax.psum_scatter(g, ("batch", "seq"), scatter_dimension=0, tiled=True).astype(jnp.float32)
+            for g in grads
+        ]
+    sum_qkv, sum_gains, sum_out, sum_wide, sum_narrow = sums
     return (
         outputs,
         grad_tokens,
-        shards[:, :first_end],
-        shards[:, first_end:second_end],
-        shards[:, second_end:third_end],
-        shards[:, third_end:fourth_end],
-        shards[:, fourth_end],
-        shards[:, fourth_end + 1],
+        sum_qkv,
+        sum_out,
+        jnp.concatenate([sum_wide[:, :FF], sum_wide[:, PADDED : PADDED + FF]], axis=1),
+        sum_narrow[:, :FF],
+        sum_gains[:, 0],
+        sum_gains[:, 1],
     )
 
 

time: 1580 us -> 508 us (0.32)
  waiting for transfers between devices: 1190 us -> 5.33 us
  Pallas kernels: 0 us -> 239 us
  local copies, waits for them, and re-layouts: 135 us -> 72 us
  blocking collectives: 41.8 us -> 0 us
    reduce_scatter x1 -> x0, waiting for transfers between devices: 1030 us -> none  [body(): lax.psum_scatter(joined, ('batch', 'seq'), scatter_dimension=0, tiled=True)]
    pallas_call x0 -> x2, Pallas kernels: none -> 239 us  [the longest x1 123 us: scatter_grads(): pl.pallas_call(functools.partial(scatter_kernel, shapes), out_shape=tuple...]
    all_gather x4 -> x0, waiting for transfers between devices: 150 us -> none  [the longest x1 77.3 us: body(): lax.all_gather(wide_weight, ('batch', 'seq'), axis=0, tiled=True)]
    concatenate x1 -> x0, local copies, waits for them, and re-layouts: 57.7 us -> none  [body(): jnp.concatenate([grad_qkv, grad_out_weight, grad_wide, grad_narrow, grad_...]
    unnamed x1 -> x0, blocking collectives: 41.8 us -> none
  transfers between devices with their start and end apart: 11 -> 6, of which waited for: 6 -> 1; matrix products, arithmetic and copies ran while one was open for 6% -> 5% of each run, Pallas kernels for 0% -> 0%
where the time goes in v1:
time: 508 us; the launch traced here: 498 us
  Pallas kernels  239 us (47%)
  matrix products  115 us (23%)
  local copies, waits for them, and re-layouts  72 us (14%)
  other arithmetic  47.7 us (9%)
  starting transfers between devices  16.3 us (3%)
  waiting for transfers between devices  5.33 us (1%)
    pallas_call x1, Pallas kernels, scatter_grads(): pl.pallas_call(functools.partial(scatter_kernel, shapes), out_shape=tuple...  123 us
    pallas_call x1, Pallas kernels, gather_weights(): pl.pallas_call(gather_kernel, out_shape=tuple((jax.ShapeDtypeStruct((2, 2...  116 us
    dot_general x1, matrix products, body(): jnp.einsum('nd,df->nf', cot_low, narrow_full, preferred_element_type=jnp....  17.6 us
    unnamed x103, local copies, waits for them, and re-layouts  16.1 us
    ppermute x3, starting transfers between devices, with_halo(): before = lax.ppermute(last, axis, up)  12.5 us
    another operation x6, other arithmetic  12 us
    dot_general x1, matrix products, body(): jnp.einsum('nd,nf->df', second_low, grad_expanded, preferred_element_type...  11.7 us
    dot_general x1, matrix products, body(): jnp.einsum('nf,df->nd', grad_expanded, wide_full, preferred_element_type=...  11.6 us
  transfers between devices with their start and end apart: 6, of which 1 were waited for; matrix products, arithmetic and copies ran while one was open for 5% of the time, Pallas kernels for 0%

profile of v1, /device:TPU:0, one launch (start us, length us, event | category | flops | bytes accessed | tf_op | source)
XLA Modules:
  0.0 498.4 jit_solution(1198168377979143898)
XLA Ops:
  5.8 116.1 %shard_map.161 = (bf16[2,2,2,128,3072]{4,3,2,1,0:T(8,128)(2,1)S(1)}, bf16[2,2,2,128,128]{4,3,2,1,0:T(8,128)(2,1)S(1)}, bf16[2,2,2,128,1024]{4,3,2,1,0:T(8,128)(2...) custom-call(bf16[32,3072]{1,0:T(8,128)(2,1)S(1)} %copy-done.1, ...), custom_call_target="tpu_custom_call" | custom-call | tf_op jit(solution)/shard_map/pallas_call | solution.py:331
  131.1 8.7 %copy.60 = bf16[3072,1024]{1,0:T(8,128)(2,1)} copy(bf16[3072,1024]{0,1:T(8,128)(2,1)} %bitcast.227) | data formatting | bytes 12582912 | tf_op jit(solution)/shard_map/dot_general | solution.py:541
  140.2 6.6 %fusion.75 = f32[2,256,3,16,64]{1,4,3,2,0:T(8,128)S(1)} fusion(bf16[3,16,64,1024,1]{3,2,1,0,4:T(8,128)(2,1)} %bitcast.251, bf16[2,256,1024]{2,1,0:T(8,128)(2,1)S(1)} %fusion.63), kind=kOutput, calls=%fused_computation.141 | convolution fusion | flops 3221225472 | bytes 13631488 | tf_op jit(solution)/shard_map/dot_general | solution.py:541
  150.3 3.8 subtract_convert_fusion.2
  158.4 2.8 collective-permute-start
  164.9 4.5 collective-permute-start.2
  174.7 5.3 %collective-permute-done.3 = bf16[1,2,64]{2,1,0:T(2,128)(2,1)S(1)} collective-permute-done((bf16[1,2,64]{2,1,0:T(2,128)(2,1)S(1)}, bf16[1,2,64]{2,1,0:T(2,128)(2,1)S(1)}, u32[]{:S(2)}, u32[]{:S(2)}) %collective-permute-start.3) | collective-permute-done | bytes 288 | tf_op jit(solution)/shard_map/ppermute | solution.py:412
  185.1 3.9 pad_maximum_fusion.5
  191.0 16.2 %while.26 = (s32[]{:T(128)}, bf16[2,256,16,64]{1,3,2,0:T(8,128)(2,1)}, f32[2,16,256,1]{2,1,3,0:T(8,128)S(1)}, bf16[2,384,16,64]{1,3,2,0:T(8,128)(2,1)}, pred[2,2...) while((s32[]{:T(128)}, ...), condition=%wide.region_5.6_spmd, body=%wide.region_2.5_spmd.sunk | while | flops 424931328 | bytes 28412024 | solution.py:571
  195.5 3.7 fusion.132
  203.6 3.7 fusion.132
  207.3 2.7 copy.66
  212.0 9.3 %fusion.90 = f32[512,5376]{1,0:T(8,128)S(1)} fusion(bf16[1024,5376]{1,0:T(8,128)(2,1)} %bitcast.279, f32[512,1024]{1,0:T(8,128)S(1)} %get-tuple-element.263, f32[1024]{0:T(1024)S(1)} %bitcast.271, f32[512]{0:T(512)S(1)} %add_rsqrt_fusion, f32[512]{0:T(512)S(1)} %broadcast_multiply_fusion.4), kind=kOutput, calls=%fused_computation.191 | convolution fusion | flops 5639241728 | bytes 24125440 | tf_op jit(solution)/shard_map/dot_general | solution.py:577
  221.3 17.6 %add_convert_fusion = (bf16[512,2688]{1,0:T(8,128)(2,1)}, f32[512,2688]{1,0:T(8,128)S(1)}, f32[2688,512]{0,1:T(8,128)}) fusion(f32[512,5376]{1,0:T(8,128)S(1)} %fusion.90, bf16[512,1024]{1,0:T(8,128)(2,1)S(1)} %bitcast.264, bf16[1024,2688]{1,0:T(8,128)(2,1)S(1)} %bitcast.238), kind=kOutput, calls=%fused_computation.72 | convolution fusion | flops 2919038976 | bytes 31326208 | tf_op jit(solution)/shard_map/nd,df->nf/dot_general | solution.py:586
  238.9 5.0 fusion.46
  243.9 11.7 %convolution_convert_fusion = bf16[1024,5376]{1,0:T(8,128)(2,1)} fusion(bf16[512,2688]{1,0:T(8,128)(2,1)} %get-tuple-element.220, bf16[512,2688]{1,0:T(8,128)(2,1)} %get-tuple-element.214, f32[512,1024]{1,0:T(8,128)S(1)} %get-tuple-element.263, f32[1024]{0:T(1024)S(1)} %bitcast.272, f32[512]{0:T(512)S(1)} %add_rsqrt_fusion, f32[512]{0:T(512)S(1)} %broadcast_multiply_fusion.4), kind=kOutput, calls=%fused_computation.55 | convolution fusion | flops 5655756800 | bytes 18620416 | tf_op jit(solution)/shard_map/nd,nf->df/dot_general | solution.py:591
  255.6 11.6 %multiply_reduce_fusion.1 = (bf16[1024]{0:T(1024)(128)(2,1)S(1)}, f32[512]{0:T(512)S(1)}, f32[512]{0:T(512)S(1)}, f32[512,1024]{1,0:T(8,128)S(1)}) fusion(f32[512,1024]{1,0:T(8,128)S(1)} %get-tuple-element.263, f32[512]{0:T(512)S(1)} %add_rsqrt_fusion, f32[512]{0:T(512)S(1)} %broadcast_multiply_fusion.4, f32[1024]{0:T(1024)S(1)} %bitcast.273, ...), kind=kOutput, calls=%fused_computation.124 | convolution fusion | flops 5652346880 | bytes 20723712 | tf_op jit(solution)/shard_map/nf,df->nd/dot_general | solution.py:594
  272.9 2.8 copy.70
  275.7 24.4 %while.27 = (s32[]{:T(128)}, f32[2,256,16,64]{1,3,2,0:T(8,128)}, f32[2,384,16,64]{1,3,2,0:T(8,128)}, f32[2,384,16,64]{1,3,2,0:T(8,128)}, bf16[2,384,16,64]{1,3,2...) while((s32[]{:T(128)}, f32[2,256,16,64]{1,3,2,0:T(8,128)}, ...), condition=%wide.region_12.13_spmd, body=%wide.region_10.12_spmd.sunk | while | flops 1023012864 | bytes 108647720 | solution.py:607
  276.2 3.2 exponential_select_fusion.3
  288.1 3.2 exponential_select_fusion.3
  300.1 3.3 fusion.56
  311.4 5.1 %collective-permute-start.4 = (bf16[2,2,64,1024]{3,2,1,0:T(8,128)(2,1)}, bf16[2,2,64,1024]{3,2,1,0:T(8,128)(2,1)}, u32[]{:S(2)}, u32[]{:S(2)}) collective-permute-start(bf16[2,2,64,1024]{3,2,1,0:T(8,128)(2,1)} %copy.71), channel_id=1, source_target_pairs={{0,1},{1,2},{2,3},{4,5},{5,6},{6,7},{8,9},{9,10},{10,11},{12,13},{... | collective-permute-start | bytes 1572872 | tf_op jit(solution)/shard_map/ppermute | solution.py:411
  320.2 7.7 %add_convert_fusion.1 = bf16[512,1024]{1,0:T(8,128)(2,1)} fusion(f32[512,1024]{1,0:T(8,128)S(1)} %copy-done.17, bf16[512,2688]{1,0:T(8,128)(2,1)} %get-tuple-element.221, bf16[1024,2688]{1,0:T(8,128)(2,1)} %bitcast.235), kind=kOutput, calls=%fused_computation.127 | convolution fusion | flops 2819620864 | bytes 11403264 | tf_op jit(solution)/shard_map/nf,df->nd/dot_general | solution.py:581
  327.9 5.1 %convolution_convert_fusion.1 = bf16[2688,1024]{0,1:T(8,128)(2,1)} fusion(bf16[512,2688]{1,0:T(8,128)(2,1)S(1)} %copy-done.28, bf16[512,1024]{1,0:T(8,128)(2,1)S(1)} %bitcast.265), kind=kOutput, calls=%fused_computation.65 | convolution fusion | flops 2821324800 | bytes 9306112 | tf_op jit(solution)/shard_map/nd,nf->df/dot_general | solution.py:587
  337.0 2.7 maximum_convert_fusion
  339.7 2.9 fusion.55
  347.2 3.3 copy.75
  351.8 5.5 %fusion.73 = (bf16[1024]{0:T(1024)(128)(2,1)S(1)}, f32[512]{0:T(512)S(1)}, f32[512]{0:T(512)S(1)}, f32[512,1024]{1,0:T(8,128)}) fusion(bf16[2,256,1024]{2,1,0:T(8,128)(2,1)S(1)} %copy-done.13, f32[512]{0:T(512)S(1)} %bitcast.277, f32[512]{0:T(512)S(1)} %bitcast.275, f32[1024]{0:T(1024)S(1)} %bitcast.269, bf16[512,3072]{0,1:T(8,128)(2,1)S(1)} %bitcast.258, ...), kind=kOutput, calls=%fused_computation.123 | convolution fusion | flops 3225942016 | bytes 12597248 | tf_op jit(solution)/shard_map/ne,de->nd/dot_general | solution.py:639
  358.3 7.3 %convolution_convert_fusion.2 = bf16[1024,3072]{1,0:T(8,128)(2,1)} fusion(bf16[512,1024]{1,0:T(8,128)(2,1)S(1)} %bitcast.263, bf16[512,3072]{0,1:T(8,128)(2,1)} %bitcast.259), kind=kOutput, calls=%fused_computation.66 | convolution fusion | flops 3224371200 | bytes 10485760 | tf_op jit(solution)/shard_map/nd,ne->de/dot_general | solution.py:636
  365.6 123.0 %shard_map.162 = (f32[32,3072]{1,0:T(8,128)}, f32[32,128]{1,0:T(8,128)}, f32[32,1024]{1,0:T(8,128)}, f32[32,5376]{1,0:T(8,128)}, f32[32,2688]{1,0:T(8,128)}) custom-call(bf16[2,2,2,128,3072]{4,3,2,1,0:T(8,128)(2,1)} %bitcast.252, bf16[2,2,2,128,128]{4,3,2,1,0:T(8,128)(2,1)} %bitcast.262, bf16[2,2,2,128,1024]{4,3,2,1,0:T(8,128)(2,1)} %bitcast.260, ...), custom_call_target="tpu_custom_call" | custom-call | tf_op jit(solution)/shard_map/pallas_call | solution.py:379
  492.4 3.4 fusion.72
  (230 shorter events, 100.5 us)
Async XLA Ops:
  128.0 11.8 %copy-start.43 = (f32[1024,1]{0,1:T(1,128)}, f32[1024,1]{0,1:T(1,128)S(1)}, u32[]{:S(2)}) copy-start(f32[1024,1]{0,1:T(1,128)S(1)} %copy.90) | copy-start | bytes 12292
  131.1 8.7 %copy-start.11 = (bf16[2,256,1024]{2,1,0:T(8,128)(2,1)S(1)}, bf16[2,256,1024]{2,1,0:T(8,128)(2,1)}, u32[]{:S(2)}) copy-start(bf16[2,256,1024]{2,1,0:T(8,128)(2,1)} %param.14) | copy-start | bytes 3145732
  140.2 6.7 %copy-start.32 = (bf16[2,256,1024]{2,1,0:T(8,128)(2,1)}, bf16[2,256,1024]{2,1,0:T(8,128)(2,1)S(1)}, u32[]{:S(2)}) copy-start(bf16[2,256,1024]{2,1,0:T(8,128)(2,1)S(1)} %fusion.63) | copy-start | bytes 3145732
  149.3 4.9 copy-start.18
  154.2 10.6 %copy-start.47 = (s32[2,256]{1,0:T(2,128)S(1)}, s32[2,256]{1,0:T(2,128)}, u32[]{:S(2)}) copy-start(s32[2,256]{1,0:T(2,128)} %param.15) | copy-start | bytes 6148
  154.2 10.6 %copy-start.48 = (s32[2,256]{1,0:T(2,128)S(1)}, s32[2,256]{1,0:T(2,128)}, u32[]{:S(2)}) copy-start(s32[2,256]{1,0:T(2,128)} %param.16) | copy-start | bytes 6148
  158.4 22.0 %collective-permute-start = (bf16[2,2,64,1024]{3,2,1,0:T(8,128)(2,1)}, bf16[2,2,64,1024]{3,2,1,0:T(8,128)(2,1)}, u32[]{:S(2)}, u32[]{:S(2)}) collective-permute-start(bf16[2,2,64,1024]{3,2,1,0:T(8,128)(2,1)} %copy.62), channel_id=1, source_target_pairs={{0,1},{1,2},{2,3},{4,5},{5,6},{6,7},{8,9},{9,10},{10,11},{12,13},{... | collective-permute-start | bytes 1572872 | tf_op jit(solution)/shard_map/ppermute | solution.py:411
  163.5 19.2 %collective-permute-start.1 = (bf16[2,2,64,1024]{3,2,1,0:T(8,128)(2,1)}, bf16[2,2,64,1024]{3,2,1,0:T(8,128)(2,1)}, u32[]{:S(2)}, u32[]{:S(2)}) collective-permute-start(bf16[2,2,64,1024]{3,2,1,0:T(8,128)(2,1)} %copy.63), channel_id=1, source_target_pairs={{1,0},{2,1},{3,2},{5,4},{6,5},{7,6},{9,8},{10,9},{11,10},{13,12},{... | collective-permute-start | bytes 1572872 | tf_op jit(solution)/shard_map/ppermute | solution.py:412
  164.9 9.8 %collective-permute-start.2 = (bf16[1,2,64]{2,1,0:T(2,128)(2,1)S(1)}, bf16[1,2,64]{2,1,0:T(2,128)(2,1)S(1)}, u32[]{:S(2)}, u32[]{:S(2)}) collective-permute-start(bf16[1,2,64]{2,1,0:T(2,128)(2,1)S(1)} %get-tuple-element.260), channel_id=1, source_target_pairs={{0,1},{1,2},{2,3},{4,5},{5,6},{6,7},{8,9},{9,10},{10,11},{12,13},{... | collective-permute-start | bytes 776 | tf_op jit(solution)/shard_map/ppermute | solution.py:411
  169.5 10.5 %collective-permute-start.3 = (bf16[1,2,64]{2,1,0:T(2,128)(2,1)S(1)}, bf16[1,2,64]{2,1,0:T(2,128)(2,1)S(1)}, u32[]{:S(2)}, u32[]{:S(2)}) collective-permute-start(bf16[1,2,64]{2,1,0:T(2,128)(2,1)S(1)} %get-tuple-element.261), channel_id=1, source_target_pairs={{1,0},{2,1},{3,2},{5,4},{6,5},{7,6},{9,8},{10,9},{11,10},{13,12},{... | collective-permute-start | bytes 776 | tf_op jit(solution)/shard_map/ppermute | solution.py:412
  207.3 4.4 copy-start.5
  210.3 11.1 %slice-start.2 = ((s8[5505024]{0:T(1024)(128)(4,1)}), s8[4194304]{0:T(1024)(128)(4,1)S(1)}, s32[]{:S(2)}) async-start(s8[5505024]{0:T(1024)(128)(4,1)} %bitcast.236), calls=%async_computation.2 | async-start | bytes 8388608
  211.6 55.5 %copy-start.16 = (f32[512,1024]{1,0:T(8,128)}, f32[512,1024]{1,0:T(8,128)S(1)}, u32[]{:S(2)}) copy-start(f32[512,1024]{1,0:T(8,128)S(1)} %get-tuple-element.263) | copy-start | bytes 6291460
  212.0 9.3 %slice-start.3 = ((s8[5505024]{0:T(1024)(128)(4,1)}), s8[1310720]{0:T(1024)(128)(4,1)S(1)}, s32[]{:S(2)}) async-start(s8[5505024]{0:T(1024)(128)(4,1)} %bitcast.236), calls=%async_computation.3 | async-start | bytes 2621440
  212.0 9.3 %copy-start.34 = (bf16[2,256,1024]{2,1,0:T(8,128)(2,1)S(1)}, bf16[2,256,1024]{2,1,0:T(8,128)(2,1)}, u32[]{:S(2)}) copy-start(bf16[2,256,1024]{2,1,0:T(8,128)(2,1)} %param.23) | copy-start | bytes 3145732
  255.6 11.6 %copy-start.35 = (bf16[2,256,1024]{2,1,0:T(8,128)(2,1)S(1)}, bf16[2,256,1024]{2,1,0:T(8,128)(2,1)}, u32[]{:S(2)}) copy-start(bf16[2,256,1024]{2,1,0:T(8,128)(2,1)} %param.23) | copy-start | bytes 3145732
  270.5 5.1 %copy-start.4 = (bf16[2,384,16,64]{1,3,2,0:T(8,128)(2,1)S(1)}, bf16[2,384,16,64]{1,3,2,0:T(8,128)(2,1)}, u32[]{:S(2)}) copy-start(bf16[2,384,16,64]{1,3,2,0:T(8,128)(2,1)} %get-tuple-element.454) | copy-start | bytes 4718596
  300.1 3.3 copy-start.9
  308.8 11.4 %copy-start.17 = (f32[512,1024]{1,0:T(8,128)S(1)}, f32[512,1024]{1,0:T(8,128)}, u32[]{:S(2)}) copy-start(f32[512,1024]{1,0:T(8,128)} %copy-done.16) | copy-start | bytes 6291460
  311.4 21.6 %collective-permute-start.4 = (bf16[2,2,64,1024]{3,2,1,0:T(8,128)(2,1)}, bf16[2,2,64,1024]{3,2,1,0:T(8,128)(2,1)}, u32[]{:S(2)}, u32[]{:S(2)}) collective-permute-start(bf16[2,2,64,1024]{3,2,1,0:T(8,128)(2,1)} %copy.71), channel_id=1, source_target_pairs={{0,1},{1,2},{2,3},{4,5},{5,6},{6,7},{8,9},{9,10},{10,11},{12,13},{... | collective-permute-start | bytes 1572872 | tf_op jit(solution)/shard_map/ppermute | solution.py:411
  318.8 15.8 %collective-permute-start.5 = (bf16[2,2,64,1024]{3,2,1,0:T(8,128)(2,1)}, bf16[2,2,64,1024]{3,2,1,0:T(8,128)(2,1)}, u32[]{:S(2)}, u32[]{:S(2)}) collective-permute-start(bf16[2,2,64,1024]{3,2,1,0:T(8,128)(2,1)} %copy.72), channel_id=1, source_target_pairs={{1,0},{2,1},{3,2},{5,4},{6,5},{7,6},{9,8},{10,9},{11,10},{13,12},{... | collective-permute-start | bytes 1572872 | tf_op jit(solution)/shard_map/ppermute | solution.py:412
  320.2 7.7 %copy-start.28 = (bf16[512,2688]{1,0:T(8,128)(2,1)S(1)}, bf16[512,2688]{1,0:T(8,128)(2,1)}, u32[]{:S(2)}) copy-start(bf16[512,2688]{1,0:T(8,128)(2,1)} %get-tuple-element.221) | copy-start | bytes 8257540
  320.2 7.7 %copy-start.36 = (bf16[2,256,1024]{2,1,0:T(8,128)(2,1)S(1)}, bf16[2,256,1024]{2,1,0:T(8,128)(2,1)}, u32[]{:S(2)}) copy-start(bf16[2,256,1024]{2,1,0:T(8,128)(2,1)} %param.23) | copy-start | bytes 3145732
  333.0 4.0 copy-start.20
  346.8 4.4 slice-start
  347.2 4.1 slice-start.1
  351.2 6.1 %copy-start.27 = (bf16[384,8,2,256]{3,1,2,0:T(8,128)(2,1)}, bf16[384,8,2,256]{3,1,2,0:T(8,128)(2,1)S(1)}, u32[]{:S(2)}) copy-start(bf16[384,8,2,256]{3,1,2,0:T(8,128)(2,1)S(1)} %copy.88) | copy-start | bytes 9437188
  351.8 6.5 %copy-start.33 = (bf16[2,256,1024]{2,1,0:T(8,128)(2,1)S(1)}, bf16[2,256,1024]{2,1,0:T(8,128)(2,1)}, u32[]{:S(2)}) copy-start(bf16[2,256,1024]{2,1,0:T(8,128)(2,1)} %copy-done.32) | copy-start | bytes 3145732
  488.6 3.8 copy-start.24
  492.4 3.4 copy-start.37
  492.4 4.2 copy-start.42
  492.4 4.8 copy-start.38
  (34 other events, 64.6 us)

commit v2 on v1

v2 whole, which is shorter than its diff:
```python
import functools

import jax
import jax.numpy as jnp
from jax import lax
from jax.experimental import pallas as pl
from jax.experimental.pallas import tpu as pltpu
from jax.sharding import PartitionSpec as P

MESH = pl.DeviceIdType.MESH
HDIM = 64
FF = 2624
PADDED = 2688
HALF = 64
NORM_EPS = 1e-05
MASK_FILL = -1e30
ROPE_BASE = 10000.0
INV_SQRT_2PI = 0.3989422804014327

GATHER_STREAMS = (
    ("zxy", "g", 0, 128),
    ("zxy", "q", 0, 768),
    ("zyx", "q", 768, 640),
    ("yxz", "q", 1408, 128),
    ("zxy", "q", 1536, 640),
    ("zyx", "q", 2176, 640),
    ("xyz", "q", 2816, 128),
    ("yxz", "q", 2944, 128),
    ("zxy", "o", 0, 384),
    ("zyx", "o", 384, 384),
    ("yxz", "o", 768, 256),
    ("zxy", "w", 0, 640),
    ("zyx", "w", 640, 640),
    ("xyz", "w", 1280, 384),
    ("yxz", "w", 1664, 128),
    ("zxy", "w", 1792, 640),
    ("zyx", "w", 2432, 640),
    ("xyz", "w", 3072, 384),
    ("yxz", "w", 3456, 128),
    ("zxy", "w", 3584, 768),
    ("zyx", "w", 4352, 768),
    ("xyz", "w", 5120, 128),
    ("yxz", "w", 5248, 128),
    ("zxy", "n", 0, 640),
    ("zyx", "n", 640, 512),
    ("xyz", "n", 1152, 256),
    ("yxz", "n", 1408, 384),
    ("zxy", "n", 1792, 256),
    ("zyx", "n", 2048, 128),
    ("yxz", "n", 2176, 512),
)
FORWARD_ORDER = (
    0, 1, 8, 15, 22, 29, 36, 43, 50, 57, 2, 64, 71, 23, 78, 92, 44, 51, 9, 99, 120, 72, 16, 127,
    148, 93, 100, 155, 24, 30, 121, 3, 128, 149, 176, 37, 183, 204, 45, 156, 211, 10, 177, 17, 184,
    205, 25, 4, 31, 38, 52, 11, 5, 46, 18, 26, 32, 6, 39, 58, 27, 65, 73, 53, 85, 7, 212, 28, 47,
    12, 54, 48, 19, 59, 66, 79, 213, 49, 74, 86, 55, 40, 56, 80, 75, 94, 33, 87, 20, 76, 101, 13,
    60, 21, 215, 77, 95, 81, 102, 106, 67, 14, 214, 113, 122, 41, 61, 96, 103, 34, 97, 68, 42, 88,
    104, 35, 216, 217, 98, 82, 105, 218, 219, 62, 69, 89, 63, 107, 70, 114, 129, 123, 83, 108, 220,
    221, 134, 90, 115, 84, 222, 130, 91, 109, 116, 124, 141, 131, 223, 135, 150, 157, 224, 110, 117,
    125, 132, 142, 136, 162, 225, 126, 133, 143, 151, 158, 169, 178, 226, 137, 144, 163, 152, 185,
    111, 227, 118, 159, 170, 164, 228, 112, 145, 138, 153, 160, 171, 179, 229, 119, 154, 161, 186,
    190, 197, 180, 206, 165, 172, 230, 187, 231, 146, 139, 191, 198, 232, 181, 207, 173, 233, 147,
    140, 166, 188, 192, 182, 199, 234, 189, 193, 208, 235, 174, 200, 236, 194, 209, 237, 167, 175,
    238, 201, 210, 168, 239, 195, 202, 240, 241, 196, 203, 242,
)
SCATTER_STREAMS = (
    ("zxy", "n", 1792, 384),
    ("zyx", "n", 2176, 384),
    ("yxz", "n", 2560, 128),
    ("zxy", "n", 0, 768),
    ("zyx", "n", 768, 640),
    ("xyz", "n", 1408, 128),
    ("yxz", "n", 1536, 256),
    ("zxy", "w", 3584, 896),
    ("zyx", "w", 4480, 512),
    ("yxz", "w", 4992, 384),
    ("zxy", "w", 1792, 640),
    ("zyx", "w", 2432, 768),
    ("xyz", "w", 3200, 128),
    ("yxz", "w", 3328, 256),
    ("zxy", "w", 0, 512),
    ("zyx", "w", 512, 896),
    ("yxz", "w", 1408, 384),
    ("zxy", "o", 0, 512),
    ("zyx", "o", 512, 256),
    ("xyz", "o", 768, 128),
    ("yxz", "o", 896, 128),
    ("zxy", "q", 2048, 640),
    ("xyz", "q", 2688, 384),
    ("zxy", "q", 1024, 256),
    ("zyx", "q", 1280, 640),
    ("xyz", "q", 1920, 128),
    ("zxy", "q", 0, 384),
    ("zyx", "q", 384, 384),
    ("xyz", "q", 768, 128),
    ("yxz", "q", 896, 128),
    ("xyz", "g", 0, 128),
)
SCATTER_ORDER = (
    0, 7, 14, 21, 1, 28, 8, 15, 35, 42, 49, 22, 16, 29, 36, 56, 43, 17, 63, 37, 70, 44, 77, 38, 64,
    84, 91, 2, 98, 45, 9, 105, 18, 30, 23, 112, 65, 119, 3, 126, 10, 133, 19, 39, 140, 147, 50, 46,
    66, 57, 154, 4, 31, 11, 20, 161, 24, 168, 5, 175, 182, 12, 32, 189, 25, 6, 40, 67, 196, 203,
    210, 13, 85, 78, 33, 92, 26, 41, 47, 58, 34, 86, 27, 93, 48, 87, 68, 71, 113, 94, 69, 59, 51,
    114, 60, 79, 95, 106, 134, 115, 52, 61, 88, 96, 99, 53, 62, 80, 97, 54, 141, 81, 135, 120, 72,
    55, 142, 82, 155, 136, 89, 143, 100, 83, 107, 73, 90, 156, 116, 127, 101, 74, 117, 121, 137,
    157, 148, 75, 102, 108, 144, 118, 138, 169, 76, 103, 139, 109, 122, 104, 128, 176, 110, 145,
    158, 123, 162, 149, 197, 177, 111, 129, 146, 124, 204, 170, 178, 198, 159, 130, 125, 190, 205,
    131, 150, 179, 199, 160, 183, 206, 132, 163, 151, 171, 180, 207, 211, 191, 152, 172, 164, 181,
    200, 153, 208, 184, 212, 173, 165, 192, 201, 213, 209, 166, 185, 174, 202, 193, 214, 167, 186,
    194, 215, 187, 216, 195, 188,
)


def place():
    b = lax.axis_index("batch")
    z = lax.axis_index("seq")
    return b, z, b // 4, (b // 2) % 2, b % 2


def remote(src, dst, sems, i, device):
    return pltpu.make_async_remote_copy(
        src_ref=src,
        dst_ref=dst,
        send_sem=sems[0].at[i],
        recv_sem=sems[1].at[i],
        device_id=device,
        device_id_type=MESH,
    )


def piece(t, n=32):
    return pl.ds(pl.multiple_of(t * n, n), n)


def enter(direct, n_seq):
    barrier = pltpu.get_barrier_semaphore()
    b, z = lax.axis_index("batch"), lax.axis_index("seq")

    def greet(device):
        pl.semaphore_signal(barrier, inc=1, device_id=device, device_id_type=MESH)

    if direct:
        for bit in (1, 2, 4):
            greet((b ^ bit, z))
    pl.when(z < n_seq - 1)(lambda: greet((b, z + 1)))
    pl.when(z > 0)(lambda: greet((b, z - 1)))
    near = (z < n_seq - 1).astype(jnp.int32) + (z > 0).astype(jnp.int32)
    pl.semaphore_wait(barrier, near + (3 if direct else 0))


class Tasks:
    def __init__(self):
        self.steps, self.names, self.finals, self.semaphores = [], [], [], 0

    def take(self, count=1):
        first = self.semaphores
        self.semaphores += count
        return first

    def add(self, name, step):
        self.names.append(name)
        self.steps.append(step)

    def run(self, order):
        for i in order:
            self.steps[i]()
        for final in self.finals:
            final()


def add_gather(tasks, streams, shards, fulls, sems):
    b, z, y, x, c = place()

    def one(j, order, name, first, count):
        full, cols = fulls[name], pl.ds(first, count)
        whole = set()

        def view(at=None, other=None):
            yy = slice(None) if "y" in whole else (1 - y if other == "y" else y)
            xx = slice(None) if "x" in whole else (1 - x if other == "x" else x)
            zz = piece(z if at is None else at) if "z" not in whole else slice(None)
            return full.at[yy, xx, c, zz, cols]

        pending, sub = None, 0
        for axis in order:
            own = None if whole else shards[name].at[:, cols]
            if axis in "xy":
                i, device = tasks.take(), (b ^ (2 if axis == "x" else 4), z)
                out = remote(view() if own is None else own, view(), sems, i, device)
                into = remote(view(other=axis), view(other=axis), sems, i, device)

                def step(pending=pending, out=out):
                    if pending:
                        pending()
                    out.start()

                tasks.add(f"g{j}.{sub}", step)
                tasks.finals.append(out.wait_send)
                pending, sub = into.wait_recv, sub + 1
            else:
                for hop in range(3):
                    i = tasks.take(2)
                    has_up, has_down = (z >= hop) & (z < 3), (z + hop <= 3) & (z > 0)
                    up_piece, down_piece = jnp.maximum(z - hop, 0), jnp.minimum(z + hop, 3)
                    above, below = (b, jnp.minimum(z + 1, 3)), (b, jnp.maximum(z - 1, 0))
                    start = own if hop == 0 else None
                    up = remote(view(up_piece) if start is None else start, view(up_piece), sems, i, above)
                    down = remote(
                        view(down_piece) if start is None else start, view(down_piece), sems, i + 1, below
                    )
                    from_below, from_above = z - 1 - hop >= 0, z + 1 + hop <= 3
                    low, high = jnp.maximum(z - 1 - hop, 0), jnp.minimum(z + 1 + hop, 3)
                    rise = remote(view(low), view(low), sems, i, above)
                    fall = remote(view(high), view(high), sems, i + 1, below)

                    def step(pending=pending, up=up, down=down, has_up=has_up, has_down=has_down):
                        if pending:
                            pending()
                        pl.when(has_up)(up.start)
                        pl.when(has_down)(down.start)

                    def pending(rise=rise, fall=fall, from_below=from_below, from_above=from_above):
                        pl.when(from_below)(rise.wait_recv)
                        pl.when(from_above)(fall.wait_recv)

                    def final(up=up, down=down, has_up=has_up, has_down=has_down):
                        pl.when(has_up)(up.wait_send)
                        pl.when(has_down)(down.wait_send)

                    tasks.add(f"g{j}.{sub}", step)
                    tasks.finals.append(final)
                    sub += 1
            whole.add(axis)
        i, device = tasks.take(), (b ^ 1, z)
        out = remote(full.at[:, :, c, :, cols], full.at[:, :, c, :, cols], sems, i, device)
        into = remote(full.at[:, :, 1 - c, :, cols], full.at[:, :, 1 - c, :, cols], sems, i, device)

        def step(pending=pending, out=out):
            pending()
            out.start()

        tasks.add(f"g{j}.{sub}", step)
        tasks.add(f"g{j}.{sub + 1}", into.wait_recv)
        tasks.finals.append(out.wait_send)

    for j, stream in enumerate(streams):
        one(j, *stream)


def dot(a, b):
    return jnp.dot(a, b, preferred_element_type=jnp.float32)


def dot_rows(a, b):
    return lax.dot_general(a, b, (((1,), (1,)), ((), ())), preferred_element_type=jnp.float32)


def dot_columns(a, b):
    return lax.dot_general(a, b, (((0,), (0,)), ((), ())), preferred_element_type=jnp.float32)


def tile(j, n):
    return pl.ds(pl.multiple_of(j * n, n), n)


def norm_parts(values):
    center = values - jnp.mean(values, -1, keepdims=True)
    inverse = lax.rsqrt(jnp.mean(center * center, -1, keepdims=True) + NORM_EPS)
    return center * inverse, inverse


def norm_rows(source, gain, target, n=64):
    @pl.loop(0, source.shape[0] // n)
    def _(i):
        unit, _ = norm_parts(source[tile(i, n), :].astype(jnp.float32))
        target[tile(i, n), :] = (unit * gain).astype(jnp.bfloat16)


def lanes(n):
    return lax.broadcasted_iota(jnp.int32, (n, 128), 1)


def rotate(u, cosine, sine):
    partner = jnp.where(lanes(u.shape[0]) % HDIM < HDIM // 2, pltpu.roll(u, 96, 1), pltpu.roll(u, 32, 1))
    return u * cosine + partner * sine


def pair_rows(block):
    zero, first = jnp.zeros_like(block), lanes(block.shape[0]) < HDIM
    return jnp.concatenate([jnp.where(first, block, zero), jnp.where(first, zero, block)], 0)


def weight_tile(full, cols):
    block = full[:, :, :, :, cols]
    return block.reshape(1024, block.shape[-1])


def forward_kernel(direct, n_seq, *refs):
    names = ("g", "q", "o", "w", "n")
    shards, refs = dict(zip(names, refs[:5])), refs[5:]
    tokens, cotangent, cosine, sine, tag_center, tag_edge, query_tag = refs[:7]
    refs = refs[7:]
    saved_names = ("q", "o", "w", "n", "normed", "queries", "keys", "values", "probs", "attended", "middle", "second")
    saved_names += ("slopes", "active", "own", "other", "gains")
    saved, refs = dict(zip(saved_names, refs[:17])), refs[17:]
    fulls, refs = dict(zip(names, refs[:5])), refs[5:]
    normed, queries, keys, values, probs, attended, middle, second, slopes, active, own, other, gains = refs[:13]
    flipped, bias, tag_prev, tag_next, send_sems, recv_sems, local_sems = refs[13:]
    sems = (send_sems, recv_sems)
    held = dict(fulls)
    held.update(normed=normed, queries=queries, keys=keys, values=values, probs=probs, attended=attended)
    held.update(middle=middle, second=second, slopes=slopes, active=active, own=own, other=other, gains=gains)
    b, z, y, x, c = place() if direct else (lax.axis_index("batch"), lax.axis_index("seq"), 0, 0, 0)
    rows, span = 2, 256
    tasks = Tasks()
    copies = {}

    def save(name):
        copies[name] = pltpu.make_async_copy(held[name], saved[name], local_sems.at[saved_names.index(name)])
        copies[name].start()

    def add_halo(name, wait_name, parts):
        (up_src, up_dst), (down_src, down_dst) = parts
        i = tasks.take(2)
        up = remote(up_src, up_dst, sems, i, (b, jnp.minimum(z + 1, n_seq - 1)))
        down = remote(down_src, down_dst, sems, i + 1, (b, jnp.maximum(z - 1, 0)))

        def start():
            pl.when(z < n_seq - 1)(up.start)
            pl.when(z > 0)(down.start)

        def wait():
            pl.when(z > 0)(up.wait_recv)
            pl.when(z < n_seq - 1)(down.wait_recv)

        def final():
            pl.when(z < n_seq - 1)(up.wait_send)
            pl.when(z > 0)(down.wait_send)

        tasks.finals.append(final)
        tasks.add(name, start)
        return wait

    wait_tags = add_halo("tags", None, ((tag_edge, tag_prev), (tag_edge, tag_next)))
    if direct:
        add_gather(tasks, GATHER_STREAMS, shards, fulls, sems)

    def edge_parts(ext):
        return (
            (ext.at[:, pl.ds(span, HALF), :], ext.at[:, pl.ds(0, HALF), :]),
            (ext.at[:, pl.ds(HALF, HALF), :], ext.at[:, pl.ds(span + HALF, HALF), :]),
        )

    def prepare():
        for k in range(8):
            place_at = (k // 2) + 4 * jnp.where(c == k % 2, 0, 1)
            flipped[tile(place_at, 128), :] = cotangent[:, k * 128 : (k + 1) * 128].T
        for ext in (keys, values):
            @pl.when(z == 0)
            def _():
                ext[:, 0:HALF, :] = jnp.zeros((rows, HALF, 1024), jnp.bfloat16)

            @pl.when(z == n_seq - 1)
            def _():
                ext[:, span + HALF :, :] = jnp.zeros((rows, HALF, 1024), jnp.bfloat16)

        @pl.when(z == 0)
        def _():
            tag_prev[...] = jnp.zeros_like(tag_prev)

        @pl.when(z == n_seq - 1)
        def _():
            tag_next[...] = jnp.zeros_like(tag_next)

    def gain_rows():
        columns = weight_tile(fulls["g"], slice(None)).astype(jnp.float32)
        gains[...] = columns.T[:8]
        save("gains")

    def first_norm():
        norm_rows(tokens, gains[0:1, :], normed)
        save("normed")

    def project(first, count, put, done=None):
        def run():
            @pl.loop(first, first + count)
            def _(j):
                out = dot(normed[...], weight_tile(fulls["q"], tile(j, 256)))
                put(j, out)

            if done:
                save(done)

        return run

    def put_query(j, out):
        for half in range(2):
            for r in range(rows):
                u = out[r * span : (r + 1) * span, half * 128 : (half + 1) * 128]
                turned = rotate(u, cosine[...], sine[...]) * HDIM**-0.5
                queries[r * span : (r + 1) * span, tile(2 * j + half, 128)] = turned.astype(jnp.bfloat16)

    def put_key(j, out):
        for half in range(2):
            for r in range(rows):
                u = out[r * span : (r + 1) * span, half * 128 : (half + 1) * 128]
                turned = rotate(u, cosine[...], sine[...]).astype(jnp.bfloat16)
                keys[r, HALF : HALF + span, tile(2 * (j - 4) + half, 128)] = turned

    def put_value(j, out):
        for r in range(rows):
            values[r, HALF : HALF + span, tile(j - 8, 256)] = out[r * span : (r + 1) * span].astype(jnp.bfloat16)

    tasks.add("prep", prepare)
    tasks.add("gain", gain_rows)
    tasks.add("norm", first_norm)
    tasks.add("q", project(0, 4, put_query))
    tasks.add("k0", project(4, 2, put_key))
    tasks.add("k1", project(6, 2, put_key))
    wait_keys = add_halo("hk", None, edge_parts(keys))
    tasks.add("v", project(8, 4, put_value, "q"))
    wait_values = add_halo("hv", None, edge_parts(values))

    def wait_halo():
        wait_tags()
        wait_keys()
        wait_values()

    tasks.add("hw", wait_halo)

    def masks():
        first = lax.broadcasted_iota(jnp.int32, (8, 128), 1) < HALF
        zero = jnp.zeros((8, 128), jnp.float32)
        low = jnp.where(first, tag_prev[...], zero) + tag_center[:, 0:128]
        high = jnp.where(first, zero, tag_next[...]) + tag_center[:, 256:384]
        ext = jnp.concatenate([low, tag_center[:, 128:256], high], 1)
        offset = lax.broadcasted_iota(jnp.int32, (128, 256), 1) - lax.broadcasted_iota(jnp.int32, (128, 256), 0)
        band, self_pair = (offset >= 0) & (offset <= 2 * HALF), offset == HALF
        for r in range(rows):
            for k in range(2):
                key_tag = ext[r : r + 1, k * 128 : k * 128 + 256]
                same = key_tag == query_tag[r * span + k * 128 : r * span + (k + 1) * 128, :]
                bias[r, k] = jnp.where(band & (same | self_pair), 0.0, MASK_FILL)
        save("queries")
        save("keys")
        save("values")

    tasks.add("bias", masks)

    def attend(r, k, first):
        def run():
            row, window = slice(r * span + k * 128, r * span + (k + 1) * 128), slice(k * 128, k * 128 + 256)

            @pl.loop(first, first + 4)
            def _(p):
                cols = tile(p, 128)
                scores = dot_rows(queries[row, cols], pair_rows(keys[r, window, cols]))
                parts = []
                for h in range(2):
                    s = scores[:, h * 256 : (h + 1) * 256] + bias[r, k]
                    weights = jnp.exp(s - jnp.max(s, -1, keepdims=True))
                    parts.append((weights * (1.0 / jnp.sum(weights, -1, keepdims=True))).astype(jnp.bfloat16))
                pair = jnp.concatenate(parts, 1)
                probs[r, k, p] = pair
                attended[row, cols] = dot(pair, pair_rows(values[r, window, cols])).astype(jnp.bfloat16)

        return run

    for i in range(8):
        tasks.add(f"att{i}", attend(i // 4, (i // 2) % 2, 4 * (i % 2)))

    def project_out():
        @pl.loop(0, 4)
        def _(j):
            cols = tile(j, 256)
            middle[:, cols] = tokens[:, cols].astype(jnp.float32) + dot(attended[...], weight_tile(fulls["o"], cols))

        for name in ("o", "probs", "attended", "middle"):
            save(name)

    def second_norm():
        norm_rows(middle, gains[1:2, :], second)
        save("second")

    tasks.add("out", project_out)
    tasks.add("norm2", second_norm)

    def gated(first):
        def run():
            @pl.loop(first, first + 3)
            def _(j):
                out = dot(second[...], weight_tile(fulls["w"], tile(j, 256)))
                gate_in, gate_up = out[:, :128], out[:, 128:]
                mass = 0.5 * (1.0 + lax.erf(gate_in * 0.5**0.5))
                density = jnp.exp(-0.5 * gate_in * gate_in) * INV_SQRT_2PI
                gelu = gate_in * mass
                slope = gate_up * (mass + gate_in * density)
                slopes[:, tile(j, 256)] = jnp.concatenate([slope, gelu], 1).astype(jnp.bfloat16)
                active[:, tile(j, 128)] = (gelu * gate_up).astype(jnp.bfloat16)

            if first == 18:
                for name in ("w", "slopes", "active"):
                    save(name)

        return run

    for i in range(7):
        tasks.add(f"w{i}", gated(3 * i))

    def grad_narrow(first, count):
        def run():
            def part(cols):
                out = dot(flipped[...], active[:, cols]).astype(jnp.bfloat16)
                own[:, cols], other[:, cols] = out[:512], out[512:]

            pl.loop(first, first + count)(lambda j: part(tile(j, 256)))
            if first + count == 10:
                part(pl.ds(2560, 128))
                save("own")
                save("other")

        return run

    for i, (first, count) in enumerate(((0, 3), (3, 3), (6, 2), (8, 2))):
        tasks.add(f"gn{i}", grad_narrow(first, count))

    if direct:
        local = [
            pltpu.make_async_copy(shards[n], fulls[n].at[y, x, c, piece(z), :], local_sems.at[17 + i])
            for i, n in enumerate(names)
        ]
    else:
        local = [pltpu.make_async_copy(shards[n], fulls[n], local_sems.at[17 + i]) for i, n in enumerate(names)]
    for copy in local:
        copy.start()
    enter(direct, n_seq)
    for copy in local:
        copy.wait()
    FORWARD_NAMES[:] = tasks.names
    tasks.run(FORWARD_ORDER if direct else range(len(tasks.steps)))
    save("n")
    for copy in copies.values():
        copy.wait()


FORWARD_NAMES = []


def forward(direct, n_seq, shards, tokens, cotangent, cosine, sine, tag_center, tag_edge, query_tag):
    bf, f32 = jnp.bfloat16, jnp.float32
    shapes = {
        "q": ((2, 2, 2, 128, 3072), bf),
        "o": ((2, 2, 2, 128, 1024), bf),
        "w": ((2, 2, 2, 128, 2 * PADDED), bf),
        "n": ((2, 2, 2, 128, PADDED), bf),
        "normed": ((512, 1024), bf),
        "queries": ((512, 1024), bf),
        "keys": ((2, 384, 1024), bf),
        "values": ((2, 384, 1024), bf),
        "probs": ((2, 2, 8, 128, 512), bf),
        "attended": ((512, 1024), bf),
        "middle": ((512, 1024), f32),
        "second": ((512, 1024), bf),
        "slopes": ((512, 2 * PADDED), bf),
        "active": ((512, PADDED), bf),
        "own": ((512, PADDED), bf),
        "other": ((512, PADDED), bf),
        "gains": ((8, 1024), f32),
    }
    vmem, anywhere = pl.BlockSpec(memory_space=pltpu.VMEM), pl.BlockSpec(memory_space=pl.ANY)
    full = [pltpu.VMEM((2, 2, 2, 128, 128), bf)] + [pltpu.VMEM(*shapes[n]) for n in ("q", "o", "w", "n")]
    rest = [pltpu.VMEM(*s) for n, s in shapes.items() if n not in ("q", "o", "w", "n")]
    out = pl.pallas_call(
        functools.partial(forward_kernel, direct, n_seq),
        out_shape=tuple(jax.ShapeDtypeStruct(*s) for s in shapes.values()),
        in_specs=[vmem if direct else anywhere] * 5 + [vmem] * 7,
        out_specs=(anywhere,) * len(shapes),
        scratch_shapes=full
        + rest
        + [
            pltpu.VMEM((1024, 512), bf),
            pltpu.VMEM((2, 2, 128, 256), f32),
            pltpu.VMEM((8, 128), f32),
            pltpu.VMEM((8, 128), f32),
            pltpu.SemaphoreType.DMA((400 if direct else 16,)),
            pltpu.SemaphoreType.DMA((400 if direct else 16,)),
            pltpu.SemaphoreType.DMA((24,)),
        ],
        compiler_params=pltpu.CompilerParams(collective_id=1, has_side_effects=True, vmem_limit_bytes=62 << 20),
    )(*shards, tokens, cotangent, cosine, sine, tag_center, tag_edge, query_tag)
    return dict(zip(shapes, out))


class Counter:
    def __init__(self): self.n=0
    def take(self,k=1):
        r=self.n; self.n+=k; return r

def add_into(dst, a, b, rows, width):
    def body(r):
        s=pl.ds(pl.multiple_of(r*16,16),16)
        dst[s,:]=a[s,:]+b[s,:]
    if rows<=32:
        for r in range(rows//16): body(r)
    else:
        pl.loop(0,rows//16)(body)

def scatter_steps(streams, grads, acc, bufs, outs, ssem, rsem, ctr):
    b,z,y,x,c=place()
    out=[]; finals=[]
    def rdma(src,dst,i,dev):
        return pltpu.make_async_remote_copy(src,dst,ssem.at[i],rsem.at[i],device_id=dev,device_id_type=MESH)
    def one(j,order,name,c0,cn):
        G=grads[name]; A=acc[name]; cols=pl.ds(c0,cn); B=bufs[j]; O=outs[name]
        steps=[]
        i=ctr.take(); dev=(b^1,z)
        cp=rdma(G.at[:,:,1-c,:,cols],B['c'],i,dev)
        steps.append(cp.start); finals.append(cp.wait_send)
        def pending(cp=cp):
            cp.wait_recv()
            for yy in range(2):
                for xx in range(2):
                    add_into(A.at[yy,xx,:,cols],A.at[yy,xx,:,cols],B['c'].at[yy,xx],128,cn)
        whole={'x','y','z'}
        def idx(fix, zz=None):
            return A.at[fix.get('y',slice(None)),fix.get('x',slice(None)),(pl.ds(pl.multiple_of(zz*32,32),32) if zz is not None else fix.get('z',slice(None))),cols]
        fix={}
        rev=order[::-1]
        for n,d in enumerate(rev):
            last=n==2
            if d in 'xy':
                i=ctr.take(); mine=y if d=='y' else x
                dev=(b^(2 if d=='x' else 4), z)
                f_other=dict(fix); f_other[d]=1-mine
                f_own=dict(fix); f_own[d]=mine
                cp=rdma(idx(f_other),B[d],i,dev)
                def fn(pending=pending,cp=cp):
                    pending(); cp.start()
                steps.append(fn); finals.append(cp.wait_send)
                def pending(cp=cp,f_own=f_own,d=d,last=last):
                    cp.wait_recv()
                    dst=idx(f_own)
                    if last:
                        O[:,cols]=dst[...].astype(jnp.float32)+B[d][...].astype(jnp.float32)
                    elif len(dst.shape)==2: add_into(dst,dst,B[d],dst.shape[0],cn)
                    else:
                        for q in range(2): add_into(dst.at[q],dst.at[q],B[d].at[q],dst.shape[1],cn)
                fix=f_own
            else:
                lead=[q for q in 'yx' if q not in fix]
                def acc_add(t,buf,fix=fix,lead=lead):
                    dst=idx(fix,t); s=pl.ds(pl.multiple_of(t*32,32),32)
                    if not lead: add_into(dst,dst,buf.at[s],32,cn)
                    elif len(lead)==2:
                        for yy in range(2):
                            for xx in range(2): add_into(dst.at[yy,xx],dst.at[yy,xx],buf.at[yy,xx,s],32,cn)
                    else:
                        for q in range(2): add_into(dst.at[q],dst.at[q],buf.at[q,s],32,cn)
                def bat(buf,t,lead=lead):
                    return buf.at[tuple([slice(None)]*len(lead))+(pl.ds(pl.multiple_of(t*32,32),32),)]
                prev=None
                for h in (2,1,0):
                    i=ctr.take(2)
                    td=jnp.maximum(z-1-h,0); tu=jnp.minimum(z+1+h,3)
                    cd=z-1-h>=0; cu=z+1+h<=3
                    dn=rdma(idx(fix,td),bat(B['d'],td),i,(b,jnp.maximum(z-1,0)))
                    up=rdma(idx(fix,tu),bat(B['u'],tu),i+1,(b,jnp.minimum(z+1,3)))
                    rd=jnp.logical_and(z<3, z-h>=0); ru=jnp.logical_and(z>0, z+h<=3)
                    rtd=jnp.maximum(z-h,0); rtu=jnp.minimum(z+h,3)
                    wd=rdma(idx(fix,rtd),bat(B['d'],rtd),i,(b,jnp.maximum(z-1,0)))
                    wu=rdma(idx(fix,rtu),bat(B['u'],rtu),i+1,(b,jnp.minimum(z+1,3)))
                    def fn(pending=pending,up=up,dn=dn,cu=cu,cd=cd):
                        pending()
                        pl.when(cd)(dn.start); pl.when(cu)(up.start)
                    steps.append(fn)
                    def fin(up=up,dn=dn,cu=cu,cd=cd):
                        pl.when(cd)(dn.wait_send); pl.when(cu)(up.wait_send)
                    finals.append(fin)
                    def pending(wd=wd,wu=wu,rd=rd,ru=ru,rtd=rtd,rtu=rtu,acc_add=acc_add):
                        @pl.when(rd)
                        def _():
                            wd.wait_recv(); acc_add(rtd,B['d'])
                        @pl.when(ru)
                        def _():
                            wu.wait_recv(); acc_add(rtu,B['u'])
                fix=dict(fix); fix['z']=pl.ds(pl.multiple_of(z*32,32),32)
                if last:
                    def pending(pending=pending,fix=fix):
                        pending()
                        O[:,cols]=idx(fix)[...].astype(jnp.float32)
        steps.append(pending)
        out.append(steps)
    for j,s in enumerate(streams): one(j,*s)
    return out, finals

def landing(streams):
    res=[]
    for (order,name,c0,cn) in streams:
        d={'c':(2,2,128,cn)}
        have={'x':2,'y':2}; zr=128
        for q in order[::-1]:
            if q in 'xy':
                del have[q]
                d[q]=tuple(have.values())+(zr,cn)
            else:
                d['d']=tuple(have.values())+(128,cn); d['u']=d['d']; zr=32
        res.append(d)
    return res


WIDTHS = {"q": 3072, "g": 128, "o": 1024, "w": 2 * PADDED, "n": PADDED}
NAMES = tuple(WIDTHS)


def scatter_kernel(shapes, *refs):
    count = len(NAMES)
    grads = dict(zip(NAMES, refs[:count]))
    outs = dict(zip(NAMES, refs[count : 2 * count]))
    acc = dict(zip(NAMES, refs[2 * count : 3 * count]))
    rest = list(refs[3 * count :])
    bufs = []
    for s in shapes:
        bufs.append(dict(zip(s, rest[: len(s)])))
        rest = rest[len(s) :]
    ssem, rsem, lsem = rest
    b, z, y, x, c = place()
    local = [
        pltpu.make_async_copy(grads[n].at[:, :, c], acc[n], lsem.at[i]) for i, n in enumerate(NAMES)
    ]
    for copy in local:
        copy.start()
    enter(True, 4)
    steps, finals = scatter_steps(SCATTER_STREAMS, grads, acc, bufs, outs, ssem, rsem, Counter())
    flat = [f for s in steps for f in s]
    for copy in local:
        copy.wait()
    for i in SCATTER_ORDER:
        flat[i]()
    for f in finals:
        f()


def scatter_grads(*grads):
    shapes = landing(SCATTER_STREAMS)
    grads = [g.reshape(2, 2, 2, 128, g.shape[-1]) for g in grads]
    return pl.pallas_call(
        functools.partial(scatter_kernel, shapes),
        out_shape=tuple(jax.ShapeDtypeStruct((32, WIDTHS[n]), jnp.float32) for n in NAMES),
        in_specs=[pl.BlockSpec(memory_space=pl.ANY)] * len(NAMES),
        out_specs=tuple(pl.BlockSpec(memory_space=pltpu.VMEM) for n in NAMES),
        scratch_shapes=[pltpu.VMEM((2, 2, 128, WIDTHS[n]), jnp.bfloat16) for n in NAMES]
        + [pltpu.VMEM(v, jnp.bfloat16) for s in shapes for v in s.values()]
        + [
            pltpu.SemaphoreType.DMA((500,)),
            pltpu.SemaphoreType.DMA((500,)),
            pltpu.SemaphoreType.DMA((8,)),
        ],
        compiler_params=pltpu.CompilerParams(
            collective_id=2, has_side_effects=True, vmem_limit_bytes=60 << 20
        ),
    )(*grads)


def with_halo(array, sides, width):
    for axis, dim in sides:
        size, length = (lax.axis_size(axis), array.shape[dim])
        up = [(i, (i + 1) % size) for i in range(size - 1)]
        down = [(j, i) for i, j in up]
        last = lax.slice_in_dim(array, length - width, length, axis=dim)
        first = lax.slice_in_dim(array, 0, width, axis=dim)
        before = lax.ppermute(last, axis, up)
        after = lax.ppermute(first, axis, down)
        array = jnp.concatenate([before, array, after], axis=dim)
    return array


def norm_backward(upstream, unit, inverse, gain):
    scaled = upstream * gain
    grad_gain = jnp.sum(upstream * unit, 0)
    grad = inverse * (
        scaled - jnp.mean(scaled, -1, keepdims=True) - unit * jnp.mean(scaled * unit, -1, keepdims=True)
    )
    return grad, grad_gain


def attend_back_kernel(queries, keys, values, probs, grads, grad_q, grad_k, grad_v):
    for r in range(2):
        for k in range(2):
            row, window = slice(r * 256 + k * 128, r * 256 + (k + 1) * 128), slice(k * 128, k * 128 + 256)

            @pl.loop(0, 8)
            def _(p, r=r, k=k, row=row, window=window):
                cols = tile(p, 128)
                first = lanes(256) < HDIM
                upstream, pair = grads[row, cols], probs[r, k, p]
                key_pair = pair_rows(keys[r, window, cols])
                grad_p = dot_rows(upstream, pair_rows(values[r, window, cols]))
                parts = []
                for h in range(2):
                    span = slice(h * 256, (h + 1) * 256)
                    weights = pair[:, span].astype(jnp.float32)
                    inner = jnp.sum(grad_p[:, span] * weights, -1, keepdims=True)
                    parts.append((weights * (grad_p[:, span] - inner)).astype(jnp.bfloat16))
                grad_s = jnp.concatenate(parts, 1)
                grad_q[row, cols] = dot(grad_s, key_pair) * HDIM**-0.5
                back_v = dot_columns(pair, upstream)
                back_k = dot_columns(grad_s, queries[row, cols])
                back_v = jnp.where(first, back_v[:256], back_v[256:])
                back_k = jnp.where(first, back_k[:256], back_k[256:])
                if k == 0:
                    grad_k[r, window, cols], grad_v[r, window, cols] = back_k, back_v
                else:
                    for out, back in ((grad_k, back_k), (grad_v, back_v)):
                        out[r, 128:256, cols] += back[:128]
                        out[r, 256:384, cols] = back[128:]


def attend_back(*args):
    vmem, f32 = pl.BlockSpec(memory_space=pltpu.VMEM), jnp.float32
    return pl.pallas_call(
        attend_back_kernel,
        out_shape=(
            jax.ShapeDtypeStruct((512, 1024), f32),
            jax.ShapeDtypeStruct((2, 384, 1024), f32),
            jax.ShapeDtypeStruct((2, 384, 1024), f32),
        ),
        in_specs=[vmem] * 5,
        out_specs=(vmem,) * 3,
        compiler_params=pltpu.CompilerParams(vmem_limit_bytes=50 << 20),
    )(*args)


def tables(span):
    frequency = ROPE_BASE ** (-(2.0 * jnp.arange(HDIM // 2, dtype=jnp.float32)) / HDIM)
    positions = (lax.axis_index("seq") * span + jnp.arange(span, dtype=jnp.int32)).astype(jnp.float32)
    angles = positions[:, None] * frequency[None, :]
    cosine, sine = jnp.cos(angles), jnp.sin(angles)
    return jnp.concatenate([cosine] * 4, 1), jnp.concatenate([-sine, sine, -sine, sine], 1)


def interleave(wide):
    lead = wide.shape[0]
    wide = jnp.pad(wide.reshape(lead, 2, FF), ((0, 0), (0, 0), (0, PADDED - FF)))
    return wide.reshape(lead, 2, PADDED // 128, 128).swapaxes(1, 2).reshape(lead, 2 * PADDED)


def separate(wide):
    lead = wide.shape[0]
    wide = wide.reshape(lead, PADDED // 128, 2, 128).swapaxes(1, 2).reshape(lead, 2, PADDED)
    return wide[:, :, :FF].reshape(lead, 2 * FF)


def body(
    tokens,
    segment_ids,
    padding_mask,
    qkv_weight,
    out_weight,
    wide_weight,
    narrow_weight,
    first_gain,
    second_gain,
    cotangent,
):
    row_count, span, width = tokens.shape
    count = row_count * span
    n_seq = lax.axis_size("seq")
    direct = (lax.axis_size("batch"), n_seq) == (8, 4)
    gains = jnp.stack([first_gain, second_gain], axis=1)
    shards = (
        jnp.pad(gains, ((0, 0), (0, 126))),
        qkv_weight,
        out_weight,
        interleave(wide_weight),
        jnp.pad(narrow_weight, ((0, 0), (0, PADDED - FF))),
    )
    if not direct:
        shards = [
            lax.all_gather(s, ("batch", "seq"), axis=0, tiled=True).reshape(2, 2, 2, 128, s.shape[-1]) for s in shards
        ]
    tags = jnp.where(padding_mask == 1, segment_ids + 1, 0).astype(jnp.float32)
    tag_center = jnp.pad(tags, ((0, 8 - row_count), (HALF, HALF)))
    tag_edge = jnp.pad(
        jnp.concatenate([tags[:, span - HALF :], tags[:, :HALF]], 1), ((0, 8 - row_count), (0, 0))
    )
    query_tag = (segment_ids + 1).astype(jnp.float32).reshape(count, 1)
    cosine, sine = tables(span)
    hidden = tokens.reshape(count, width)
    cot_low = cotangent.reshape(count, width)
    saved = forward(direct, n_seq, shards, hidden, cot_low, cosine, sine, tag_center, tag_edge, query_tag)
    qkv_full, out_full, wide_full, narrow_full = (saved[n].reshape(1024, -1) for n in ("q", "o", "w", "n"))
    gain_one, gain_two = saved["gains"][0:1], saved["gains"][1:2]
    hidden = hidden.astype(jnp.float32)
    middle, attended = saved["middle"], saved["attended"]
    result = middle + jnp.einsum("nf,df->nd", saved["active"], narrow_full, preferred_element_type=jnp.float32)
    outputs = result.astype(jnp.bfloat16).reshape(tokens.shape)
    grad_act = jnp.dot(cot_low, narrow_full, preferred_element_type=jnp.float32)
    slopes = saved["slopes"].astype(jnp.float32).reshape(count, PADDED // 128, 2, 128)
    grad_expanded = slopes * grad_act.reshape(count, PADDED // 128, 1, 128)
    grad_expanded = grad_expanded.astype(jnp.bfloat16).reshape(count, 2 * PADDED)
    grad_wide = jnp.einsum("nd,nf->df", saved["second"], grad_expanded, preferred_element_type=jnp.float32)
    grad_second = jnp.einsum("nf,df->nd", grad_expanded, wide_full, preferred_element_type=jnp.float32)
    unit_two, inv_two = norm_parts(middle)
    grad_mid_norm, grad_gain_two = norm_backward(grad_second, unit_two, inv_two, gain_two)
    grad_middle = cot_low.astype(jnp.float32) + grad_mid_norm
    grad_branch = grad_middle.astype(jnp.bfloat16)
    grad_out = jnp.einsum("nd,ne->de", attended, grad_branch, preferred_element_type=jnp.float32)
    grad_attended = jnp.einsum("ne,de->nd", grad_branch, out_full, preferred_element_type=jnp.float32).astype(
        jnp.bfloat16
    )
    grad_q, grad_k, grad_v = attend_back(
        saved["queries"], saved["keys"], saved["values"], saved["probs"], grad_attended
    )
    stack = jnp.stack([grad_k, grad_v])
    extent = span + 2 * HALF
    outgoing = jnp.concatenate([stack[:, :, :HALF], stack[:, :, extent - HALF :]], axis=2)
    incoming = with_halo(outgoing.astype(jnp.bfloat16), (("seq", 2),), HALF).astype(outgoing.dtype)
    owned = stack[:, :, HALF : HALF + span]
    owned = jnp.concatenate(
        [
            owned[:, :, :HALF] + incoming[:, :, :HALF],
            owned[:, :, HALF : span - HALF],
            owned[:, :, span - HALF :] + incoming[:, :, 3 * HALF :],
        ],
        axis=2,
    )

    def turn_back(u):
        u = u.reshape(row_count, span, width // HDIM, 2, HDIM // 2)
        co = cosine[:, : HDIM // 2][None, :, None, :]
        si = sine[:, HDIM // 2 : HDIM][None, :, None, :]
        a, b = u[..., 0, :], u[..., 1, :]
        return jnp.stack([a * co + b * si, b * co - a * si], 3).reshape(count, width)

    grad_projected = jnp.concatenate(
        [turn_back(grad_q), turn_back(owned[0]), owned[1].reshape(count, width)], 1
    ).astype(jnp.bfloat16)
    grad_qkv = jnp.einsum("nd,ne->de", saved["normed"], grad_projected, preferred_element_type=jnp.float32)
    grad_normed = jnp.einsum("ne,de->nd", grad_projected, qkv_full, preferred_element_type=jnp.float32)
    unit_one, inv_one = norm_parts(hidden)
    grad_in_norm, grad_gain_one = norm_backward(grad_normed, unit_one, inv_one, gain_one)
    grad_tokens = (grad_middle + grad_in_norm).astype(jnp.bfloat16).reshape(tokens.shape)
    grad_gains = jnp.pad(jnp.stack([grad_gain_one, grad_gain_two], axis=1), ((0, 0), (0, 126)))
    low = [g.astype(jnp.bfloat16) for g in (grad_qkv, grad_gains, grad_out, grad_wide)]
    mine = (lax.axis_index("batch") % 2 if direct else 0) == 0
    own, other = (saved[n].reshape(4, 128, PADDED) for n in ("own", "other"))
    grad_narrow = jnp.stack([jnp.where(mine, own, other), jnp.where(mine, other, own)], 1).reshape(1024, PADDED)
    grads = low + [grad_narrow]
    if direct:
        sums = scatter_grads(*grads)
    else:
        sums = [
            lax.psum_scatter(g, ("batch", "seq"), scatter_dimension=0, tiled=True).astype(jnp.float32) for g in grads
        ]
    sum_qkv, sum_gains, sum_out, sum_wide, sum_narrow = sums
    return (
        outputs,
        grad_tokens,
        sum_qkv,
        sum_out,
        separate(sum_wide),
        sum_narrow[:, :FF],
        sum_gains[:, 0],
        sum_gains[:, 1],
    )


def solution(mesh):
    placed = (
        P("batch", "seq", None),
        P("batch", "seq"),
        P("batch", "seq"),
        P(("batch", "seq"), None),
        P(("batch", "seq"), None),
        P(("batch", "seq"), None),
        P(("batch", "seq"), None),
        P(("batch", "seq")),
        P(("batch", "seq")),
        P("batch", "seq", None),
    )
    return jax.shard_map(
        body,
        mesh=mesh,
        in_specs=placed,
        out_specs=(
            P("batch", "seq", None),
            P("batch", "seq", None),
            P(("batch", "seq"), None),
            P(("batch", "seq"), None),
            P(("batch", "seq"), None),
            P(("batch", "seq"), None),
            P(("batch", "seq")),
            P(("batch", "seq")),
        ),
        check_vma=False,
    )
```

time: 508 us -> 445 us (0.88); the launches traced: 498 us -> 442 us
  matrix products: 115 us -> 59.8 us
  Pallas kernels: 239 us -> 284 us
  other arithmetic: 47.7 us -> 30.7 us
  starting transfers between devices: 16.3 us -> 3.37 us
  local copies, waits for them, and re-layouts: 72 us -> 62.4 us
  waiting for transfers between devices: 5.33 us -> 0.01 us
    dot_general x22 -> x4, matrix products: 94.4 us -> 35.5 us  [the longest x1 11.9 us: body(): jnp.einsum('nd,nf->df', saved['second'], grad_expanded, preferred_element...]
    pallas_call x1 -> x2, Pallas kernels: 116 us -> 159 us  [the longest x1 137 us: forward(): pl.pallas_call(functools.partial(forward_kernel, direct, n_seq), out_shap...]
    mul x0 -> x3, local copies, waits for them, and re-layouts: none -> 29.3 us  [body(): grad_expanded = slopes * grad_act.reshape(count, PADDED // 128, 1, 128)]
    while x30 -> x0, local copies, waits for them, and re-layouts: 12.1 us -> none
    ppermute x3 -> x1, starting transfers between devices: 12.5 us -> 2.09 us  [with_halo(): before = lax.ppermute(last, axis, up)]
    unnamed x103 -> x62, local copies, waits for them, and re-layouts: 16.1 us -> 6.73 us
    dot_general x1 -> x0, local copies, waits for them, and re-layouts: 8.71 us -> none  [body(): jnp.dot(normed_low, qkv_full, preferred_element_type=jnp.float32)]
    ppermute x4 -> x0, local copies, waits for them, and re-layouts: 8.68 us -> none  [the longest x2 4.72 us: with_halo(): after = lax.ppermute(first, axis, down)]
  transfers between devices with their start and end apart: 6 -> 2, of which waited for: 1 -> 0; matrix products, arithmetic and copies ran while one was open for 5% -> 10% of each run, Pallas kernels for 0% -> 0%
where the time goes in v2:
time: 445 us; the launch traced here: 442 us
  Pallas kernels  284 us (64%)
  local copies, waits for them, and re-layouts  62.4 us (14%)
  matrix products  59.8 us (13%)
  other arithmetic  30.7 us (7%)
    pallas_call x1, Pallas kernels, forward(): pl.pallas_call(functools.partial(forward_kernel, direct, n_seq), out_shap...  137 us
    pallas_call x1, Pallas kernels, scatter_grads(): pl.pallas_call(functools.partial(scatter_kernel, shapes), out_shape=tuple...  124 us
    mul x3, local copies, waits for them, and re-layouts, body(): grad_expanded = slopes * grad_act.reshape(count, PADDED // 128, 1, 128)  29.3 us
    pallas_call x1, Pallas kernels, attend_back(): pl.pallas_call(attend_back_kernel, out_shape=(jax.ShapeDtypeStruct((512,...  22.5 us
    dot_general x1, matrix products, body(): jnp.einsum('nf,df->nd', grad_expanded, wide_full, preferred_element_type=...  13 us
    dot_general x1, matrix products, body(): jnp.einsum('nd,nf->df', saved['second'], grad_expanded, preferred_element...  11.9 us
  transfers between devices with their start and end apart: 2, of which 0 were waited for; matrix products, arithmetic and copies ran while one was open for 10% of the time, Pallas kernels for 0%

profile of v2, /device:TPU:0, one launch (start us, length us, event | category | flops | bytes accessed | tf_op | source)
XLA Modules:
  0.0 441.5 jit_solution(12952701120251389183)
XLA Ops:
  3.5 1.6 pad.27.refs_4_
  10.7 137.0 %shard_map.161 = (bf16[2,2,2,128,3072]{4,3,2,1,0:T(8,128)(2,1)}, bf16[2,2,2,128,1024]{4,3,2,1,0:T(8,128)(2,1)}, bf16[2,2,2,128,5376]{4,3,2,1,0:T(8,128)(2,1)}, b...) custom-call(bf16[32,128]{1,0:T(8,128)(2,1)} %pad.25.refs_0_, ...), custom_call_target="tpu_custom_call" | custom-call | tf_op jit(solution)/shard_map/pallas_call | solution.py:573
  147.7 7.6 %fusion.21 = f32[2688,512]{1,0:T(8,128)} fusion(bf16[1024,2688]{1,0:T(8,128)(2,1)} %bitcast.114, bf16[512,1024]{1,0:T(8,128)(2,1)S(1)} %bitcast.90), kind=kOutput, calls=%fused_computation.85 | convolution fusion | flops 2818572288 | bytes 12058624 | tf_op jit(solution)/shard_map/dot_general | solution.py:897
  156.7 6.3 %copy.47 = f32[512,21,128]{2,1,0:T(8,128)} copy(f32[512,21,128]{0,2,1:T(8,128)} %bitcast.85) | data formatting | bytes 11010048 | tf_op jit(solution)/shard_map/mul | solution.py:899
  163.1 8.6 %mul.198 = f32[512,21,2,128]{3,2,1,0:T(2,128)} broadcast(f32[512,21,128]{2,1,0:T(8,128)} %copy.47), dimensions={0,1,3} | broadcast | bytes 16515072 | tf_op jit(solution)/shard_map/mul | solution.py:899
  171.7 14.3 %mul.199 = f32[512,5376]{1,0:T(8,128)} reshape(f32[512,21,2,128]{3,2,1,0:T(2,128)} %mul.198) | data formatting | bytes 22020096 | tf_op jit(solution)/shard_map/mul | solution.py:899
  186.0 13.0 %multiply_reduce_fusion = (bf16[1024]{0:T(1024)(128)(2,1)S(1)}, f32[512]{0:T(512)S(1)}, f32[512]{0:T(512)S(1)}, f32[512,1024]{1,0:T(8,128)S(1)}) fusion(f32[512,1024]{1,0:T(8,128)S(1)} %copy-done.5, f32[512]{0:T(512)S(1)} %add_rsqrt_fusion, f32[512]{0:T(512)S(1)} %broadcast_multiply_fusion.5, f32[1024]{0:T(1024)S(1)} %bitcast.101, ...), kind=kOutput, calls=%fused_computation.22 | convolution fusion | flops 5649594368 | bytes 31733760 | tf_op jit(solution)/shard_map/nf,df->nd/dot_general | solution.py:902
  202.3 22.5 %shard_map.162 = (f32[512,1024]{1,0:T(8,128)}, f32[2,384,1024]{2,1,0:T(8,128)}, f32[2,384,1024]{2,1,0:T(8,128)}) custom-call(bf16[512,1024]{1,0:T(8,128)(2,1)S(1)} %copy-done.1, bf16[2,384,1024]{2,1,0:T(8,128)(2,1)S(1)} %copy-done, bf16[2,384,1024]{2,1,0:T(8,128)(2,1)} %get-tuple-element.41.values, bf16[2,2,8,128,512]{4,3,2,1,0:T(8,128)(2,1)} %get-tuple-element.42.probs, ...), custom_call_target="tpu_custom_call" | custom-call | tf_op jit(solution)/shard_map/pallas_call | solution.py:820
  224.8 3.4 fusion
  229.3 2.1 collective-permute-start
  233.3 8.4 %add_convert_fusion.1 = bf16[512,1024]{1,0:T(8,128)(2,1)} fusion(f32[512,1024]{1,0:T(8,128)} %get-tuple-element.33, bf16[512,2688]{1,0:T(8,128)(2,1)} %get-tuple-element.34, bf16[1024,2688]{1,0:T(8,128)(2,1)} %bitcast.115), kind=kOutput, calls=%fused_computation.30 | convolution fusion | flops 2819620864 | bytes 11403264 | tf_op jit(solution)/shard_map/nf,df->nd/dot_general | solution.py:895
  241.7 11.9 %convolution_convert_fusion = bf16[1024,5376]{1,0:T(8,128)(2,1)} fusion(bf16[512,1024]{1,0:T(8,128)(2,1)} %get-tuple-element.50, f32[512,5376]{1,0:T(8,128)S(1)} %bitcast.73, bf16[512,5376]{1,0:T(8,128)(2,1)} %get-tuple-element.36), kind=kOutput, calls=%fused_computation | convolution fusion | flops 5650907136 | bytes 28573696 | tf_op jit(solution)/shard_map/nd,nf->df/dot_general | solution.py:901
  253.6 4.6 %convolution_convert_fusion.2 = bf16[1024,1024]{1,0:T(8,128)(2,1)} fusion(bf16[512,1024]{1,0:T(8,128)(2,1)} %get-tuple-element.49, f32[512,1024]{1,0:T(8,128)} %copy-done.9), kind=kOutput, calls=%fused_computation.32 | convolution fusion | flops 1075314688 | bytes 5242880 | tf_op jit(solution)/shard_map/nd,ne->de/dot_general | solution.py:907
  258.3 3.3 broadcast_select_fusion.1
  261.6 1.5 copy-done.3
  263.1 1.5 fusion.3
  264.8 2.9 copy.48
  267.7 3.5 reshape.270
  271.2 5.7 %pad_maximum_fusion.1.refs_4_ = bf16[2,2,2,128,2688]{4,3,2,1,0:T(8,128)(2,1)} fusion(bf16[2,2,1,128,2688]{4,3,2,1,0:T(8,128)(2,1)} %bitcast.82, bf16[2,2,1,128,2688]{4,3,2,1,0:T(8,128)(2,1)} %bitcast.81), kind=kLoop, calls=%fused_computation.11 | loop fusion | flops 2752512 | bytes 11010048 | tf_op jit(solution)/shard_map/stack | solution.py:947
  276.9 1.7 fusion.6
  279.8 1.8 copy.51
  283.0 1.8 fusion.18
  284.8 2.8 add_convert_fusion.3
  287.6 1.4 pad_maximum_fusion.6
  289.3 1.4 pad_maximum_fusion.7
  291.0 5.4 %multiply_reduce_fusion.1 = (bf16[1024]{0:T(1024)(128)(2,1)S(1)}, f32[512]{0:T(512)S(1)}, f32[512]{0:T(512)S(1)}, f32[512,1024]{1,0:T(8,128)}) fusion(f32[512]{0:T(512)S(1)} %bitcast.107, f32[512]{0:T(512)S(1)} %bitcast.105, bf16[2,256,1024]{2,1,0:T(8,128)(2,1)S(1)} %copy-done.7, f32[1024]{0:T(1024)S(1)} %bitcast.103, bf16[1024,3072]{1,0:T(8,128)(2,1)S(1)} %bitcast.113, ...), kind=kOutput, calls=%fused_computation.23 | convolution fusion | flops 3235379200 | bytes 12597248 | tf_op jit(solution)/shard_map/ne,de->nd/dot_general | solution.py:939
  297.4 7.6 %convolution_convert_fusion.1 = bf16[1024,3072]{1,0:T(8,128)(2,1)} fusion(bf16[512,1024]{1,0:T(8,128)(2,1)} %get-tuple-element.48, bf16[512,1024]{0,1:T(8,128)(2,1)S(1)} %copy-done.15, bf16[512,1024]{0,1:T(8,128)(2,1)} %bitcast.97, bf16[512,1024]{0,1:T(8,128)(2,1)S(1)} %bitcast.95), kind=kOutput, calls=%fused_computation.10 | convolution fusion | flops 3233808384 | bytes 10485760 | tf_op jit(solution)/shard_map/nd,ne->de/dot_general | solution.py:938
  305.0 124.2 %shard_map.163 = (f32[32,3072]{1,0:T(8,128)}, f32[32,128]{1,0:T(8,128)}, f32[32,1024]{1,0:T(8,128)}, f32[32,5376]{1,0:T(8,128)}, f32[32,2688]{1,0:T(8,128)}) custom-call(bf16[2,2,2,128,3072]{4,3,2,1,0:T(8,128)(2,1)} %bitcast.84, bf16[2,2,2,128,128]{4,3,2,1,0:T(8,128)(2,1)} %bitcast.93, bf16[2,2,2,128,1024]{4,3,2,1,0:T(8,128)(2,1)} %bitcast.92, ...), custom_call_target="tpu_custom_call" | custom-call | tf_op jit(solution)/shard_map/pallas_call | solution.py:746
  429.3 1.6 slice_reduce_fusion
  430.9 2.3 reshape.279
  433.1 2.4 reshape.281
  435.6 3.4 add_convert_fusion
  (106 shorter events, 22.4 us)
Async XLA Ops:
  7.6 140.1 %copy-start.12 = (bf16[2,256,1024]{2,1,0:T(8,128)(2,1)S(1)}, bf16[2,256,1024]{2,1,0:T(8,128)(2,1)}, u32[]{:S(2)}) copy-start(bf16[2,256,1024]{2,1,0:T(8,128)(2,1)} %param.19) | copy-start | bytes 3145732
  147.7 7.6 %copy-start.5 = (f32[512,1024]{1,0:T(8,128)S(1)}, f32[512,1024]{1,0:T(8,128)}, u32[]{:S(2)}) copy-start(f32[512,1024]{1,0:T(8,128)} %get-tuple-element.33) | copy-start | bytes 6291460
  199.0 1.6 copy-start.20
  199.8 2.1 copy-start.9
  200.6 1.4 copy-start
  200.6 1.7 copy-start.1
  228.2 4.4 %copy-start.6 = (bf16[2,256,1024]{2,1,0:T(8,128)(2,1)S(1)}, bf16[2,256,1024]{2,1,0:T(8,128)(2,1)}, u32[]{:S(2)}) copy-start(bf16[2,256,1024]{2,1,0:T(8,128)(2,1)} %param.10) | copy-start | bytes 3145732
  229.3 47.7 %collective-permute-start = (bf16[2,2,64,1024]{3,2,1,0:T(8,128)(2,1)}, bf16[2,2,64,1024]{3,2,1,0:T(8,128)(2,1)}, u32[]{:S(2)}, u32[]{:S(2)}) collective-permute-start(bf16[2,2,64,1024]{3,2,1,0:T(8,128)(2,1)} %get-tuple-element.70), channel_id=1, source_target_pairs={{0,1},{1,2},{2,3},{4,5},{5,6},{6,7},{8,9},{9,10},{10,11},{12,13},{... | collective-permute-start | bytes 1572872 | tf_op jit(solution)/shard_map/ppermute | solution.py:771
  231.4 45.6 %collective-permute-start.1 = (bf16[2,2,64,1024]{3,2,1,0:T(8,128)(2,1)}, bf16[2,2,64,1024]{3,2,1,0:T(8,128)(2,1)}, u32[]{:S(2)}, u32[]{:S(2)}) collective-permute-start(bf16[2,2,64,1024]{3,2,1,0:T(8,128)(2,1)} %get-tuple-element.71), channel_id=1, source_target_pairs={{1,0},{2,1},{3,2},{5,4},{6,5},{7,6},{9,8},{10,9},{11,10},{13,12},{... | collective-permute-start | bytes 1572872 | tf_op jit(solution)/shard_map/ppermute | solution.py:772
  232.9 8.8 %slice-start = ((s8[11010048]{0:T(1024)(128)(4,1)}), s8[4194304]{0:T(1024)(128)(4,1)S(1)}, s32[]{:S(2)}) async-start(s8[11010048]{0:T(1024)(128)(4,1)} %bitcast.72), calls=%async_computation | async-start | bytes 8388608
  233.3 8.4 %slice-start.1 = ((s8[11010048]{0:T(1024)(128)(4,1)}), s8[4194304]{0:T(1024)(128)(4,1)S(1)}, s32[]{:S(2)}) async-start(s8[11010048]{0:T(1024)(128)(4,1)} %bitcast.72), calls=%async_computation.1 | async-start | bytes 8388608
  233.3 8.4 %slice-start.2 = ((s8[11010048]{0:T(1024)(128)(4,1)}), s8[2621440]{0:T(1024)(128)(4,1)S(1)}, s32[]{:S(2)}) async-start(s8[11010048]{0:T(1024)(128)(4,1)} %bitcast.72), calls=%async_computation.2 | async-start | bytes 5242880
  253.6 4.6 %copy-start.13 = (bf16[512,2688]{1,0:T(8,128)(2,1)S(1)}, bf16[512,2688]{1,0:T(8,128)(2,1)}, u32[]{:S(2)}) copy-start(bf16[512,2688]{1,0:T(8,128)(2,1)} %get-tuple-element.51) | copy-start | bytes 8257540
  253.6 4.6 %copy-start.14 = (bf16[512,2688]{1,0:T(8,128)(2,1)S(1)}, bf16[512,2688]{1,0:T(8,128)(2,1)}, u32[]{:S(2)}) copy-start(bf16[512,2688]{1,0:T(8,128)(2,1)} %get-tuple-element.52) | copy-start | bytes 8257540
  258.2 3.3 copy-start.2
  258.3 4.8 %copy-start.3 = (f32[2,384,1024]{2,1,0:T(8,128)S(1)}, f32[2,384,1024]{2,1,0:T(8,128)}, u32[]{:S(2)}) copy-start(f32[2,384,1024]{2,1,0:T(8,128)} %get-tuple-element.46) | copy-start | bytes 9437188
  271.2 5.7 %copy-start.4 = (f32[2,384,1024]{2,1,0:T(8,128)S(1)}, f32[2,384,1024]{2,1,0:T(8,128)}, u32[]{:S(2)}) copy-start(f32[2,384,1024]{2,1,0:T(8,128)} %get-tuple-element.46) | copy-start | bytes 9437188
  276.9 1.9 copy-start.11
  281.7 3.2 copy-start.8
  283.0 8.0 %slice-start.3 = ((s8[6291456]{0:T(1024)(128)(4,1)}), s8[4194304]{0:T(1024)(128)(4,1)S(1)}, s32[]{:S(2)}) async-start(s8[6291456]{0:T(1024)(128)(4,1)} %bitcast.111), calls=%async_computation.3 | async-start | bytes 8388608
  284.8 6.1 %slice-start.4 = ((s8[6291456]{0:T(1024)(128)(4,1)}), s8[2097152]{0:T(1024)(128)(4,1)S(1)}, s32[]{:S(2)}) async-start(s8[6291456]{0:T(1024)(128)(4,1)} %bitcast.111), calls=%async_computation.4 | async-start | bytes 4194304
  289.0 1.9 copy-start.7
  289.0 1.9 copy-start.15
  290.9 5.5 %copy-start.16 = (bf16[128,8,2,256]{3,1,2,0:T(8,128)(2,1)}, bf16[128,8,2,256]{3,1,2,0:T(8,128)(2,1)S(1)}, u32[]{:S(2)}) copy-start(bf16[128,8,2,256]{3,1,2,0:T(8,128)(2,1)S(1)} %copy.63) | copy-start | bytes 3145732
  429.3 6.3 %copy-start.10 = (f32[512,1024]{1,0:T(8,128)S(1)}, f32[512,1024]{1,0:T(8,128)}, u32[]{:S(2)}) copy-start(f32[512,1024]{1,0:T(8,128)} %copy-done.9) | copy-start | bytes 6291460
  435.6 3.4 copy-start.17
  435.6 4.1 copy-start.19
  435.6 4.8 %copy-start.18 = (f32[32,2688]{1,0:T(8,128)S(1)}, f32[32,2688]{1,0:T(8,128)}, u32[]{:S(2)}) copy-start(f32[32,2688]{1,0:T(8,128)} %get-tuple-element.56) | copy-start | bytes 1032196

commit v3 on v2

v3 whole, which is shorter than its diff:
```python
import functools
from typing import Any, NamedTuple

import jax
import jax.numpy as jnp
from jax import lax
from jax.experimental import pallas as pl
from jax.experimental.pallas import tpu as pltpu
from jax.sharding import PartitionSpec as P

MESH = pl.DeviceIdType.MESH
HDIM = 64
FF = 2624
PADDED = 2688
HALF = 64
BATCH, SEQ = "batch", "seq"
ORDERS = ("zxy", "zyx", "xyz", "yxz")
FULL = ("g", "q", "o", "w", "n")
NORM_EPS = 1e-05
MASK_FILL = -1e30
ROPE_BASE = 10000.0
INV_SQRT_2PI = 0.3989422804014327

GATHER_STREAMS = (
    (0, 0, 0, 128),
    (0, 1, 0, 512),
    (1, 1, 512, 512),
    (0, 1, 1024, 512),
    (1, 1, 1536, 512),
    (0, 1, 2048, 512),
    (1, 1, 2560, 512),
    (0, 2, 0, 512),
    (1, 2, 512, 512),
    (0, 4, 0, 640),
    (1, 4, 640, 640),
    (2, 4, 1280, 128),
    (3, 4, 1408, 128),
    (0, 4, 1536, 512),
    (1, 4, 2048, 512),
    (3, 4, 2560, 128),
    (0, 3, 0, 640),
    (1, 3, 640, 640),
    (2, 3, 1280, 128),
    (3, 3, 1408, 128),
    (0, 3, 1536, 640),
    (1, 3, 2176, 640),
    (2, 3, 2816, 128),
    (3, 3, 2944, 128),
    (0, 3, 3072, 640),
    (1, 3, 3712, 640),
    (2, 3, 4352, 128),
    (3, 3, 4480, 128),
    (0, 3, 4608, 384),
    (1, 3, 4992, 384),
)
FORWARD_ORDER = (
    0, 1, 8, 15, 22, 29, 78, 85, 36, 106, 127, 43, 134, 211, 2, 155, 162, 183, 190, 9, 79, 86, 16,
    107, 128, 135, 23, 30, 50, 37, 156, 163, 57, 3, 184, 44, 64, 71, 10, 17, 191, 24, 4, 31, 38, 45,
    11, 5, 80, 92, 18, 99, 87, 25, 6, 32, 51, 113, 120, 58, 12, 7, 65, 212, 39, 19, 72, 213, 108,
    26, 52, 59, 33, 81, 46, 66, 73, 129, 88, 13, 93, 141, 148, 53, 40, 20, 14, 100, 136, 67, 82, 21,
    214, 60, 89, 157, 27, 83, 169, 176, 94, 34, 109, 90, 114, 164, 101, 47, 74, 28, 215, 121, 84,
    197, 204, 54, 35, 216, 91, 185, 95, 110, 41, 217, 115, 192, 61, 68, 42, 48, 130, 102, 49, 218,
    111, 55, 122, 116, 112, 219, 75, 96, 137, 62, 56, 142, 149, 63, 158, 220, 221, 222, 69, 131,
    123, 117, 103, 165, 223, 138, 76, 132, 170, 143, 177, 150, 70, 139, 224, 133, 159, 97, 144, 225,
    140, 77, 186, 104, 151, 124, 166, 160, 98, 226, 193, 171, 105, 167, 198, 145, 161, 205, 227,
    178, 168, 118, 172, 228, 187, 152, 125, 229, 194, 179, 188, 119, 230, 126, 195, 199, 206, 173,
    189, 231, 146, 200, 196, 232, 233, 207, 153, 180, 147, 234, 201, 235, 236, 154, 237, 238, 174,
    239, 240, 208, 181, 241, 175, 202, 242, 182, 243, 244, 245, 209, 203, 246, 247, 248, 210, 249,
    250, 251, 252, 253, 254, 255, 256, 257, 258, 259, 260,
)
SCATTER_CHUNKS = (
    (4, 0, 1536),
    (4, 1536, 1152),
    (3, 0, 1536),
    (3, 1536, 1536),
    (3, 3072, 1536),
    (3, 4608, 768),
    (2, 0, 1024),
    (1, 0, 1024),
    (1, 1024, 1024),
    (1, 2048, 1024),
)
SCATTER_STREAMS = (
    (0, 4, 0, 768),
    (1, 4, 768, 768),
    (0, 4, 1536, 512),
    (1, 4, 2048, 512),
    (3, 4, 2560, 128),
    (0, 3, 0, 768),
    (1, 3, 768, 768),
    (0, 3, 1536, 768),
    (1, 3, 2304, 768),
    (0, 3, 3072, 768),
    (1, 3, 3840, 768),
    (0, 3, 4608, 384),
    (1, 3, 4992, 384),
    (0, 2, 0, 512),
    (1, 2, 512, 512),
    (0, 1, 0, 512),
    (1, 1, 512, 512),
    (0, 1, 1024, 512),
    (1, 1, 1536, 512),
    (0, 1, 2048, 512),
    (1, 1, 2560, 512),
)
BACKWARD_ORDER = (
    31, 33, 0, 1, 2, 3, 32, 51, 57, 35, 4, 34, 63, 69, 75, 37, 5, 76, 6, 36, 81, 87, 77, 39, 7, 38,
    41, 8, 40, 52, 58, 42, 10, 64, 70, 11, 78, 93, 99, 12, 13, 14, 53, 59, 15, 82, 88, 54, 65, 71,
    79, 16, 60, 55, 105, 111, 20, 17, 61, 66, 72, 18, 80, 19, 56, 83, 89, 67, 94, 73, 100, 9, 117,
    123, 43, 24, 84, 90, 45, 22, 85, 21, 62, 106, 112, 91, 44, 68, 74, 95, 101, 129, 135, 46, 23,
    102, 96, 86, 103, 25, 97, 118, 124, 92, 141, 147, 47, 26, 107, 104, 113, 49, 108, 27, 114, 48,
    98, 109, 115, 153, 159, 28, 130, 119, 125, 136, 50, 110, 120, 29, 126, 116, 121, 142, 127, 148,
    30, 165, 171, 122, 131, 137, 128, 154, 160, 138, 132, 149, 139, 143, 133, 150, 144, 151, 145,
    140, 134, 166, 172, 161, 152, 155, 146, 162, 156, 173, 163, 167, 157, 174, 168, 175, 169, 164,
    158, 176, 170,
)


def place():
    b = lax.axis_index(BATCH)
    z = lax.axis_index(SEQ)
    return b, z, b // 4, (b // 2) % 2, b % 2


def remote(src, dst, sems, i, device):
    return pltpu.make_async_remote_copy(
        src_ref=src,
        dst_ref=dst,
        send_sem=sems[0].at[i],
        recv_sem=sems[1].at[i],
        device_id=device,
        device_id_type=MESH,
    )


def piece(t, n=32):
    return pl.ds(pl.multiple_of(t * n, n), n)


def enter(direct, n_seq):
    barrier = pltpu.get_barrier_semaphore()
    b, z = lax.axis_index(BATCH), lax.axis_index(SEQ)

    def greet(device):
        pl.semaphore_signal(barrier, inc=1, device_id=device, device_id_type=MESH)

    if direct:
        for bit in (1, 2, 4):
            greet((b ^ bit, z))
    pl.when(z < n_seq - 1)(lambda: greet((b, z + 1)))
    pl.when(z > 0)(lambda: greet((b, z - 1)))
    near = (z < n_seq - 1).astype(jnp.int32) + (z > 0).astype(jnp.int32)
    pl.semaphore_wait(barrier, near + (3 if direct else 0))


class Tasks:
    def __init__(self):
        self.steps, self.finals, self.semaphores = [], [], 0

    def take(self, count=1):
        first = self.semaphores
        self.semaphores += count
        return first

    def add(self, step):
        self.steps.append(step)

    def run(self, order):
        for i in order:
            self.steps[i]()
        for final in self.finals:
            final()


def add_gather(tasks, streams, shards, fulls, sems):
    b, z, y, x, c = place()

    def one(j, order, name, first, count):
        full, cols = fulls[name], pl.ds(first, count)
        whole = set()

        def view(at=None, other=None):
            yy = slice(None) if "y" in whole else (1 - y if other == "y" else y)
            xx = slice(None) if "x" in whole else (1 - x if other == "x" else x)
            zz = piece(z if at is None else at) if "z" not in whole else slice(None)
            return full.at[yy, xx, c, zz, cols]

        pending, sub = None, 0
        for axis in order:
            own = None if whole else shards[name].at[:, cols]
            if axis in "xy":
                i, device = tasks.take(), (b ^ (2 if axis == "x" else 4), z)
                out = remote(view() if own is None else own, view(), sems, i, device)
                into = remote(view(other=axis), view(other=axis), sems, i, device)

                def step(pending=pending, out=out):
                    if pending:
                        pending()
                    out.start()

                tasks.add(step)
                tasks.finals.append(out.wait_send)
                pending, sub = into.wait_recv, sub + 1
            else:
                for hop in range(3):
                    i = tasks.take(2)
                    has_up, has_down = (z >= hop) & (z < 3), (z + hop <= 3) & (z > 0)
                    up_piece, down_piece = jnp.maximum(z - hop, 0), jnp.minimum(z + hop, 3)
                    above, below = (b, jnp.minimum(z + 1, 3)), (b, jnp.maximum(z - 1, 0))
                    start = own if hop == 0 else None
                    up = remote(view(up_piece) if start is None else start, view(up_piece), sems, i, above)
                    down = remote(
                        view(down_piece) if start is None else start, view(down_piece), sems, i + 1, below
                    )
                    from_below, from_above = z - 1 - hop >= 0, z + 1 + hop <= 3
                    low, high = jnp.maximum(z - 1 - hop, 0), jnp.minimum(z + 1 + hop, 3)
                    rise = remote(view(low), view(low), sems, i, above)
                    fall = remote(view(high), view(high), sems, i + 1, below)

                    def step(pending=pending, up=up, down=down, has_up=has_up, has_down=has_down):
                        if pending:
                            pending()
                        pl.when(has_up)(up.start)
                        pl.when(has_down)(down.start)

                    def pending(rise=rise, fall=fall, from_below=from_below, from_above=from_above):
                        pl.when(from_below)(rise.wait_recv)
                        pl.when(from_above)(fall.wait_recv)

                    def final(up=up, down=down, has_up=has_up, has_down=has_down):
                        pl.when(has_up)(up.wait_send)
                        pl.when(has_down)(down.wait_send)

                    tasks.add(step)
                    tasks.finals.append(final)
                    sub += 1
            whole.add(axis)
        i, device = tasks.take(), (b ^ 1, z)
        out = remote(full.at[:, :, c, :, cols], full.at[:, :, c, :, cols], sems, i, device)
        into = remote(full.at[:, :, 1 - c, :, cols], full.at[:, :, 1 - c, :, cols], sems, i, device)

        def step(pending=pending, out=out):
            pending()
            out.start()

        tasks.add(step)
        tasks.add(into.wait_recv)
        tasks.finals.append(out.wait_send)

    for j, (order, which, first, count) in enumerate(streams):
        one(j, ORDERS[order], FULL[which], first, count)


def dot(a, b):
    return jnp.dot(a, b, preferred_element_type=jnp.float32)


def dot_rows(a, b):
    return lax.dot_general(a, b, (((1,), (1,)), ((), ())), preferred_element_type=jnp.float32)


def dot_columns(a, b):
    return lax.dot_general(a, b, (((0,), (0,)), ((), ())), preferred_element_type=jnp.float32)


def tile(j, n):
    return pl.ds(pl.multiple_of(j * n, n), n)


def norm_parts(values):
    center = values - jnp.mean(values, -1, keepdims=True)
    inverse = lax.rsqrt(jnp.mean(center * center, -1, keepdims=True) + NORM_EPS)
    return center * inverse, inverse


def norm_rows(source, gain, target, n=64):
    @pl.loop(0, source.shape[0] // n)
    def _(i):
        unit, _ = norm_parts(source[tile(i, n), :].astype(jnp.float32))
        target[tile(i, n), :] = (unit * gain).astype(jnp.bfloat16)


def lanes(n):
    return lax.broadcasted_iota(jnp.int32, (n, 128), 1)


def rotate(u, cosine, sine):
    partner = jnp.where(lanes(u.shape[0]) % HDIM < HDIM // 2, pltpu.roll(u, 96, 1), pltpu.roll(u, 32, 1))
    return u * cosine + partner * sine


def pair_rows(block):
    zero, first = jnp.zeros_like(block), lanes(block.shape[0]) < HDIM
    return jnp.concatenate([jnp.where(first, block, zero), jnp.where(first, zero, block)], 0)


def weight_tile(full, cols):
    block = full[:, :, :, :, cols]
    return block.reshape(1024, block.shape[-1])


def flip(source, target, c):
    for k in range(8):
        at = (k // 2) + 4 * jnp.where(c == k % 2, 0, 1)
        target[tile(at, 128), :] = source[:, k * 128 : (k + 1) * 128].T


def edge_exchange(tasks, sems, n_seq, up_src, up_dst, down_src, down_dst):
    b, z = lax.axis_index(BATCH), lax.axis_index(SEQ)
    i = tasks.take(2)
    up = remote(up_src, up_dst, sems, i, (b, jnp.minimum(z + 1, n_seq - 1)))
    down = remote(down_src, down_dst, sems, i + 1, (b, jnp.maximum(z - 1, 0)))

    def start():
        pl.when(z < n_seq - 1)(up.start)
        pl.when(z > 0)(down.start)

    def wait():
        pl.when(z > 0)(up.wait_recv)
        pl.when(z < n_seq - 1)(down.wait_recv)

    def final():
        pl.when(z < n_seq - 1)(up.wait_send)
        pl.when(z > 0)(down.wait_send)

    tasks.finals.append(final)
    return start, wait


HELD = ("normed", "queries", "keys", "values", "probs", "attended", "middle", "gains", "flip_normed", "flip_attended")


def forward_kernel(direct, n_seq, *refs):
    refs = list(refs)

    def pop(names):
        return {n: refs.pop(0) for n in names}

    shards = pop(FULL)
    tokens, cotangent, cosine, sine, tag_center, tag_edge, query_tag = pop(range(7)).values()
    saved = Saved(*[refs.pop(0) for _ in Saved._fields])
    fulls = pop(FULL)
    held = pop(HELD)
    normed, queries, keys, values, probs, attended, middle, gains, flip_normed, flip_attended = held.values()
    second, flip_second, flip_cotangent, total, final, active, upstream, bias, tag_prev, tag_next = pop(range(10)).values()
    expanded_ring, narrow_ring, wide_ring = pop(range(3)).values()
    send_sems, recv_sems, local_sems, ring_sems = refs
    sems = (send_sems, recv_sems)
    held.update(fulls)
    b, z, y, x, c = place() if direct else (lax.axis_index(BATCH), lax.axis_index(SEQ), 0, 0, 0)
    rows, span = 2, 256
    tasks = Tasks()
    copies = {}

    def save(name):
        target = getattr(saved, name)
        copies[name] = pltpu.make_async_copy(held[name], target, local_sems.at[Saved._fields.index(name)])
        copies[name].start()

    start_tags, wait_tags = edge_exchange(tasks, sems, n_seq, tag_edge, tag_prev, tag_edge, tag_next)
    tasks.add(start_tags)
    if direct:
        add_gather(tasks, GATHER_STREAMS, shards, fulls, sems)

    def edges(ext):
        return (
            ext.at[:, pl.ds(span, HALF), :],
            ext.at[:, pl.ds(0, HALF), :],
            ext.at[:, pl.ds(HALF, HALF), :],
            ext.at[:, pl.ds(span + HALF, HALF), :],
        )

    def prepare():
        flip(cotangent, flip_cotangent, c)
        for ext in (keys, values):

            @pl.when(z == 0)
            def _():
                ext[:, 0:HALF, :] = jnp.zeros((rows, HALF, 1024), jnp.bfloat16)

            @pl.when(z == n_seq - 1)
            def _():
                ext[:, span + HALF :, :] = jnp.zeros((rows, HALF, 1024), jnp.bfloat16)

        @pl.when(z == 0)
        def _():
            tag_prev[...] = jnp.zeros_like(tag_prev)

        @pl.when(z == n_seq - 1)
        def _():
            tag_next[...] = jnp.zeros_like(tag_next)

    def gain_rows():
        columns = weight_tile(fulls["g"], slice(None)).astype(jnp.float32)
        gains[...] = columns.T[:8]
        save("gains")

    def first_norm():
        norm_rows(tokens, gains[0:1, :], normed)
        flip(normed, flip_normed, c)
        save("flip_normed")

    def project(first, count, put, done=None):
        def run():
            @pl.loop(first, first + count)
            def _(j):
                put(j, dot(normed[...], weight_tile(fulls["q"], tile(j, 256))))

            if done:
                save(done)

        return run

    def put_query(j, out):
        for half in range(2):
            for r in range(rows):
                u = out[r * span : (r + 1) * span, half * 128 : (half + 1) * 128]
                turned = rotate(u, cosine[...], sine[...]) * HDIM**-0.5
                queries[r * span : (r + 1) * span, tile(2 * j + half, 128)] = turned.astype(jnp.bfloat16)

    def put_key(j, out):
        for half in range(2):
            for r in range(rows):
                u = out[r * span : (r + 1) * span, half * 128 : (half + 1) * 128]
                turned = rotate(u, cosine[...], sine[...]).astype(jnp.bfloat16)
                keys[r, HALF : HALF + span, tile(2 * (j - 4) + half, 128)] = turned

    def put_value(j, out):
        for r in range(rows):
            values[r, HALF : HALF + span, tile(j - 8, 256)] = out[r * span : (r + 1) * span].astype(jnp.bfloat16)

    tasks.add(prepare)
    tasks.add(gain_rows)
    tasks.add(first_norm)
    tasks.add(project(0, 4, put_query))
    tasks.add(project(4, 2, put_key))
    tasks.add(project(6, 2, put_key))
    start_keys, wait_keys = edge_exchange(tasks, sems, n_seq, *edges(keys))
    tasks.add(start_keys)
    tasks.add(project(8, 4, put_value, "q"))
    start_values, wait_values = edge_exchange(tasks, sems, n_seq, *edges(values))
    tasks.add(start_values)

    def wait_halo():
        wait_tags()
        wait_keys()
        wait_values()

    tasks.add(wait_halo)

    def masks():
        first = lax.broadcasted_iota(jnp.int32, (8, 128), 1) < HALF
        zero = jnp.zeros((8, 128), jnp.float32)
        low = jnp.where(first, tag_prev[...], zero) + tag_center[:, 0:128]
        high = jnp.where(first, zero, tag_next[...]) + tag_center[:, 256:384]
        ext = jnp.concatenate([low, tag_center[:, 128:256], high], 1)
        offset = lax.broadcasted_iota(jnp.int32, (128, 256), 1) - lax.broadcasted_iota(jnp.int32, (128, 256), 0)
        band, self_pair = (offset >= 0) & (offset <= 2 * HALF), offset == HALF
        for r in range(rows):
            for k in range(2):
                key_tag = ext[r : r + 1, k * 128 : k * 128 + 256]
                same = key_tag == query_tag[r * span + k * 128 : r * span + (k + 1) * 128, :]
                bias[r, k] = jnp.where(band & (same | self_pair), 0.0, MASK_FILL)
        for name in ("queries", "keys", "values"):
            save(name)

    tasks.add(masks)

    def attend(r, k, first):
        def run():
            row, window = slice(r * span + k * 128, r * span + (k + 1) * 128), slice(k * 128, k * 128 + 256)

            @pl.loop(first, first + 4)
            def _(p):
                cols = tile(p, 128)
                scores = dot_rows(queries[row, cols], pair_rows(keys[r, window, cols]))
                parts = []
                for h in range(2):
                    s = scores[:, h * 256 : (h + 1) * 256] + bias[r, k]
                    weights = jnp.exp(s - jnp.max(s, -1, keepdims=True))
                    parts.append((weights * (1.0 / jnp.sum(weights, -1, keepdims=True))).astype(jnp.bfloat16))
                pair = jnp.concatenate(parts, 1)
                probs[r, k, p] = pair
                attended[row, cols] = dot(pair, pair_rows(values[r, window, cols])).astype(jnp.bfloat16)

        return run

    for i in range(8):
        tasks.add(attend(i // 4, (i // 2) % 2, 4 * (i % 2)))

    def project_out():
        @pl.loop(0, 4)
        def _(j):
            cols = tile(j, 256)
            middle[:, cols] = tokens[:, cols].astype(jnp.float32) + dot(attended[...], weight_tile(fulls["o"], cols))

        for name in ("o", "probs", "middle"):
            save(name)

    def second_norm():
        norm_rows(middle, gains[1:2, :], second)
        flip(second, flip_second, c)
        total[...] = middle[...]

    def flip_late():
        flip(attended, flip_attended, c)
        save("flip_attended")

    tasks.add(project_out)
    tasks.add(second_norm)
    tasks.add(flip_late)

    streams = {}

    def stream(name, i, source, target):
        streams[name, i] = pltpu.make_async_copy(source, target, ring_sems.at[name, i % 2])
        streams[name, i].start()

    def free(name, i):
        if (name, i) in streams:
            streams.pop((name, i)).wait()

    def gate(i):
        def run():
            free(0, i - 2)
            upstream[...] = dot(cotangent[...], weight_tile(fulls["n"], pl.ds(i * 384, 384)))

            @pl.loop(0, 3)
            def _(k):
                out = dot(second[...], weight_tile(fulls["w"], tile(3 * i + k, 256)))
                gate_in, gate_up = out[:, :128], out[:, 128:]
                mass = 0.5 * (1.0 + lax.erf(gate_in * 0.5**0.5))
                density = jnp.exp(-0.5 * gate_in * gate_in) * INV_SQRT_2PI
                gelu, above = gate_in * mass, upstream[:, tile(k, 128)]
                slope = gate_up * (mass + gate_in * density)
                expanded_ring[i % 2, :, tile(2 * k, 128)] = (above * slope).astype(jnp.bfloat16)
                expanded_ring[i % 2, :, tile(2 * k + 1, 128)] = (above * gelu).astype(jnp.bfloat16)
                active[i % 2, :, tile(k, 128)] = (gelu * gate_up).astype(jnp.bfloat16)

            stream(0, i, expanded_ring.at[i % 2], saved.grad_expanded.at[:, pl.ds(i * 768, 768)])

        return run

    def add_output(i):
        def run():
            @pl.loop(0, 2)
            def _(j):
                block = fulls["n"][j, :, :, :, pl.ds(i * 384, 384)].reshape(512, 384)
                total[:, tile(j, 512)] += dot_rows(active[i % 2], block)

            if i == 6:
                final[...] = total[...].astype(jnp.bfloat16)
                stream(3, 0, final, saved.outputs)

        return run

    def grad_narrow(i):
        def run():
            free(1, i - 2)

            @pl.loop(0, 2)
            def _(j):
                narrow_ring[i % 2, tile(j, 512), :] = dot(flip_cotangent[tile(j, 512), :], active[i % 2]).astype(jnp.bfloat16)

            stream(1, i, narrow_ring.at[i % 2], saved.grad_narrow.at[:, pl.ds(i * 384, 384)])

        return run

    def grad_wide(i):
        def run():
            free(2, i - 2)

            @pl.loop(0, 3)
            def _(k):
                part = tile(k, 256)
                wide_ring[i % 2, :, part] = dot(flip_second[...], expanded_ring[i % 2, :, part]).astype(jnp.bfloat16)

            stream(2, i, wide_ring.at[i % 2], saved.grad_wide.at[:, pl.ds(i * 768, 768)])
            if i == 6:
                save("w")

        return run

    for i in range(7):
        tasks.add(gate(i))
        tasks.add(add_output(i))
        tasks.add(grad_narrow(i))
        tasks.add(grad_wide(i))

    base = len(Saved._fields)
    if direct:
        local = [
            pltpu.make_async_copy(shards[n], fulls[n].at[y, x, c, piece(z), :], local_sems.at[base + i])
            for i, n in enumerate(FULL)
        ]
    else:
        local = [pltpu.make_async_copy(shards[n], fulls[n], local_sems.at[base + i]) for i, n in enumerate(FULL)]
    for copy in local:
        copy.start()
    enter(direct, n_seq)
    for copy in local:
        copy.wait()
    tasks.run(FORWARD_ORDER if direct else range(len(tasks.steps)))
    for copy in list(copies.values()) + list(streams.values()):
        copy.wait()


BF, F32 = jnp.bfloat16, jnp.float32
SHAPES = {
    "g": ((2, 2, 2, 128, 128), BF),
    "q": ((2, 2, 2, 128, 3072), BF),
    "o": ((2, 2, 2, 128, 1024), BF),
    "w": ((2, 2, 2, 128, 2 * PADDED), BF),
    "n": ((2, 2, 2, 128, PADDED), BF),
    "normed": ((512, 1024), BF),
    "queries": ((512, 1024), BF),
    "keys": ((2, 384, 1024), BF),
    "values": ((2, 384, 1024), BF),
    "probs": ((2, 2, 8, 128, 512), BF),
    "attended": ((512, 1024), BF),
    "middle": ((512, 1024), F32),
    "gains": ((8, 1024), F32),
    "flip_normed": ((1024, 512), BF),
    "flip_attended": ((1024, 512), BF),
    "grad_expanded": ((512, 2 * PADDED), BF),
    "grad_narrow": ((1024, PADDED), BF),
    "grad_wide": ((1024, 2 * PADDED), BF),
    "outputs": ((512, 1024), BF),
}
VMEM, ANY = pl.BlockSpec(memory_space=pltpu.VMEM), pl.BlockSpec(memory_space=pl.ANY)


def forward(direct, n_seq, shards, *inputs):
    results = Saved._fields
    count = 400 if direct else 16
    out = pl.pallas_call(
        functools.partial(forward_kernel, direct, n_seq),
        out_shape=tuple(jax.ShapeDtypeStruct(*SHAPES[n]) for n in results),
        in_specs=[VMEM if direct else ANY] * 5 + [VMEM] * len(inputs),
        out_specs=(ANY,) * len(results),
        scratch_shapes=[pltpu.VMEM(*SHAPES[n]) for n in FULL + HELD]
        + [
            pltpu.VMEM((512, 1024), BF),
            pltpu.VMEM((1024, 512), BF),
            pltpu.VMEM((1024, 512), BF),
            pltpu.VMEM((512, 1024), F32),
            pltpu.VMEM((512, 1024), BF),
            pltpu.VMEM((2, 512, 384), BF),
            pltpu.VMEM((512, 384), F32),
            pltpu.VMEM((2, 2, 128, 256), F32),
            pltpu.VMEM((8, 128), F32),
            pltpu.VMEM((8, 128), F32),
            pltpu.VMEM((2, 512, 768), BF),
            pltpu.VMEM((2, 1024, 384), BF),
            pltpu.VMEM((2, 1024, 768), BF),
            pltpu.SemaphoreType.DMA((count,)),
            pltpu.SemaphoreType.DMA((count,)),
            pltpu.SemaphoreType.DMA((len(results) + len(FULL),)),
            pltpu.SemaphoreType.DMA((4, 2)),
        ],
        compiler_params=pltpu.CompilerParams(collective_id=1, has_side_effects=True, vmem_limit_bytes=62 << 20),
    )(*shards, *inputs)
    return Saved(*out)


def add_into(target, a, b):
    count = target.shape[0]

    def part(i):
        at = pl.ds(pl.multiple_of(i * 32, 32), 32)
        target[at, :] = a[at, :] + b[at, :]

    if count == 32:
        part(0)
    else:
        pl.loop(0, count // 32)(part)


def landing_shapes(streams):
    result = []
    for order, _, _, count in streams:
        shapes, left, depth = {}, ["y", "x"], 128
        for axis in ORDERS[order][::-1]:
            if axis == "z":
                shapes["z"] = (2,) * len(left) + (160, count)
                depth = 32
            else:
                left.remove(axis)
                shapes[axis] = (2,) * len(left) + (depth, count)
        result.append(shapes)
    return result


def add_scatter(tasks, streams, chunks, sources, totals, slots, landed, sums, sems, credit):
    b, z, y, x, c = place()
    for k, (which, first, count) in enumerate(chunks):
        name, cols = FULL[which], pl.ds(first, count)
        slot = slots.at[k % 2, :, :, :, pl.ds(0, count)]
        out = remote(sources[name].at[:, :, :, cols], slot, sems, tasks.take(), (b ^ 1, z))

        def start(k=k, out=out):
            if k >= 2:
                pl.semaphore_wait(credit.at[k % 2], 1)
            out.start()

        def arrive(k=k, out=out, name=name, cols=cols, slot=slot):
            out.wait_recv()
            for yy in range(2):
                for xx in range(2):
                    total = totals[name].at[yy, xx, :, cols]
                    add_into(total, total, slot.at[yy, xx])
            if k + 2 < len(chunks):
                pl.semaphore_signal(credit.at[k % 2], inc=1, device_id=(b ^ 1, z), device_id_type=MESH)

        tasks.add(start)
        tasks.add(arrive)
        tasks.finals.append(out.wait_send)

    def one(j, order, name, first, count):
        cols, land = pl.ds(first, count), landed[j]

        def view(fixed, at=None):
            zz = fixed.get("z", slice(None)) if at is None else piece(at)
            return totals[name].at[fixed.get("y", slice(None)), fixed.get("x", slice(None)), zz, cols]

        def blocks(ref):
            if len(ref.shape) == 2:
                return [ref]
            return [r for i in range(ref.shape[0]) for r in blocks(ref.at[i])]

        def accumulate(target, source):
            for t, s in zip(blocks(target), blocks(source)):
                add_into(t, t, s)

        fixed, pending, sub = {}, None, 0
        for axis in order[::-1]:
            if axis in "xy":
                mine, device = (y if axis == "y" else x), (b ^ (2 if axis == "x" else 4), z)
                keep = dict(fixed)
                keep[axis] = mine
                give = dict(fixed)
                give[axis] = 1 - mine
                out = remote(view(give), land[axis], sems, tasks.take(), device)

                def step(pending=pending, out=out):
                    if pending:
                        pending()
                    out.start()

                def pending(out=out, keep=keep, axis=axis):
                    out.wait_recv()
                    accumulate(view(keep), land[axis])

                tasks.add(step)
                tasks.finals.append(out.wait_send)
                fixed, sub = keep, sub + 1
            else:
                left = [a for a in "yx" if a not in fixed]

                def spot(t, own_from_below):
                    at = jnp.where(own_from_below, 128, t * 32)
                    return land["z"].at[(slice(None),) * len(left) + (pl.ds(pl.multiple_of(at, 32), 32),)]

                for hop in (2, 1, 0):
                    i = tasks.take(2)
                    down_piece, up_piece = jnp.maximum(z - 1 - hop, 0), jnp.minimum(z + 1 + hop, 3)
                    has_down, has_up = z - 1 - hop >= 0, z + 1 + hop <= 3
                    below, above = (b, jnp.maximum(z - 1, 0)), (b, jnp.minimum(z + 1, 3))
                    down = remote(view(fixed, down_piece), spot(down_piece, False), sems, i, below)
                    up = remote(view(fixed, up_piece), spot(up_piece, hop == 0), sems, i + 1, above)
                    from_above, from_below = (z < 3) & (z - hop >= 0), (z > 0) & (z + hop <= 3)
                    low, high = jnp.maximum(z - hop, 0), jnp.minimum(z + hop, 3)
                    fall = remote(view(fixed, low), spot(low, False), sems, i, below)
                    rise = remote(view(fixed, high), spot(high, hop == 0), sems, i + 1, above)

                    def step(pending=pending, up=up, down=down, has_up=has_up, has_down=has_down):
                        if pending:
                            pending()
                        pl.when(has_down)(down.start)
                        pl.when(has_up)(up.start)

                    def pending(
                        fall=fall,
                        rise=rise,
                        from_above=from_above,
                        from_below=from_below,
                        low=low,
                        high=high,
                        hop=hop,
                        fixed=fixed,
                        spot=spot,
                    ):
                        @pl.when(from_above)
                        def _():
                            fall.wait_recv()
                            accumulate(view(fixed, low), spot(low, False))

                        @pl.when(from_below)
                        def _():
                            rise.wait_recv()
                            accumulate(view(fixed, high), spot(high, hop == 0))

                    def final(up=up, down=down, has_up=has_up, has_down=has_down):
                        pl.when(has_down)(down.wait_send)
                        pl.when(has_up)(up.wait_send)

                    tasks.add(step)
                    tasks.finals.append(final)
                    sub += 1
                fixed = dict(fixed)
                fixed["z"] = piece(z)

        def last(pending=pending, fixed=fixed):
            pending()
            sums[name][:, cols] = view(fixed)[...].astype(jnp.float32)

        tasks.add(last)

    for j, (order, which, first, count) in enumerate(streams):
        one(j, ORDERS[order], FULL[which], first, count)


class Scratch(NamedTuple):
    ring: Any
    expanded: Any
    second: Any
    middle: Any
    branch: Any
    flipped: Any
    keys: Any
    values: Any
    probs: Any
    projected: Any
    grad_v: Any
    edge: Any
    edge_landed: Any
    gains: Any


class Saved(NamedTuple):
    q: Any
    o: Any
    w: Any
    queries: Any
    keys: Any
    values: Any
    probs: Any
    middle: Any
    gains: Any
    flip_normed: Any
    flip_attended: Any
    grad_expanded: Any
    grad_narrow: Any
    grad_wide: Any
    outputs: Any


WEIGHTS = ("q", "o", "w", "n")


def backward_kernel(direct, n_seq, shapes, *refs):
    refs = list(refs)

    def pop(names):
        return {n: refs.pop(0) for n in names}

    src = Saved(*[refs.pop(0) for _ in Saved._fields])
    tokens, cotangent, cosine, sine = pop(range(4)).values()
    grad_tokens = refs.pop(0)
    sums = pop(WEIGHTS if direct else range(4))
    totals = pop(WEIGHTS if direct else ("q", "o"))
    others = pop(("q", "o"))
    landed = [pop(s) for s in shapes]
    slots = refs.pop(0) if direct else None
    v = Scratch(*[refs.pop(0) for _ in Scratch._fields])
    send_sems, recv_sems, local_sems, credit = refs
    sems = (send_sems, recv_sems)
    b, z, y, x, c = place() if direct else (lax.axis_index(BATCH), lax.axis_index(SEQ), 0, 0, 0)
    rows, span = 2, 256
    tasks = Tasks()
    local = {}

    def load(name, source, target):
        local[name] = pltpu.make_async_copy(source, target, local_sems.at[name])
        local[name].start()

    def wait(name):
        local.pop(name).wait()

    def load_group(i):
        cols = pl.ds(i * 768, 768)
        load(WIDE + i % 2, src.w.at[:, :, :, :, cols], v.ring.at[i % 2, :, :, :, :, pl.ds(0, 768)])
        load(EXPANDED + i % 2, src.grad_expanded.at[:, cols], v.expanded.at[i % 2])

    def grad_second(i):
        def run():
            wait(WIDE + i % 2)
            wait(EXPANDED + i % 2)

            @pl.loop(0, 2)
            def _(j):
                block = v.ring[i % 2, j, :, :, :, pl.ds(0, 768)].reshape(512, 768)
                part = dot_rows(v.expanded[i % 2], block)
                if i == 0:
                    v.second[:, tile(j, 512)] = part
                else:
                    v.second[:, tile(j, 512)] += part

            if i < 5:
                load_group(i + 2)
            elif i == 5:
                load(WIDE + 1, src.o, v.ring.at[1])
            else:
                load(WIDE, src.q.at[:, :, :, :, pl.ds(0, 1024)], v.ring.at[0])

        return run

    for i in range(7):
        tasks.add(grad_second(i))

    def norm_back(values, upstream, gain):
        unit, inverse = norm_parts(values)
        scaled = upstream * gain
        return inverse * (
            scaled - jnp.mean(scaled, -1, keepdims=True) - unit * jnp.mean(scaled * unit, -1, keepdims=True)
        )

    def second_norm_back():
        wait(MIDDLE)
        wait(GAINS)

        @pl.loop(0, 8)
        def _(i):
            at = tile(i, 64)
            grad = norm_back(v.middle[at, :], v.second[at, :], v.gains[1:2, :])
            grad = grad + cotangent[at, :].astype(jnp.float32)
            v.middle[at, :] = grad
            v.branch[at, :] = grad.astype(jnp.bfloat16)

    tasks.add(second_norm_back)

    def back_out():
        wait(WIDE + 1)

        @pl.loop(0, 4)
        def _(j):
            block = v.ring[1, j // 2, j % 2].reshape(256, 1024)
            v.projected[:, pl.ds(pl.multiple_of(2048 + j * 256, 256), 256)] = dot_rows(
                v.branch[...], block
            ).astype(jnp.bfloat16)

        load(WIDE + 1, src.q.at[:, :, :, :, pl.ds(1024, 1024)], v.ring.at[1])
        for name in (QUERIES, KEYS, VALUES):
            wait(name)

    tasks.add(back_out)

    def grad_weight(name, first, count, source):
        def run():
            if name == "o":
                wait(FLIPPED)

            @pl.loop(first, first + count)
            def _(j):
                cols = tile(j, 256)
                out = dot(v.flipped[...], source(cols)).astype(jnp.bfloat16).reshape(2, 2, 2, 128, 256)
                totals[name][:, :, :, cols], others[name][:, :, :, cols] = out[0], out[1]

            if name == "o":
                load(FLIPPED, src.flip_normed, v.flipped)
            if name == "q" and first == 0:
                pass

        return run

    tasks.add(grad_weight("o", 0, 4, lambda cols: v.branch[:, cols]))

    def attend_back(r, k, first):
        def run():
            if first == 0:
                wait(PROBS + k)
            row, window = slice(r * span + k * 128, r * span + (k + 1) * 128), slice(k * 128, k * 128 + 256)

            @pl.loop(first, first + 4)
            def _(p):
                cols = tile(p, 128)
                upper = pl.ds(pl.multiple_of(2048 + p * 128, 128), 128)
                side = lanes(256) < HDIM
                upstream, pair = v.projected[row, upper], v.probs[k, p]
                key_pair = pair_rows(v.keys[r, window, cols])
                grad_p = dot_rows(upstream, pair_rows(v.values[r, window, cols]))
                parts = []
                for h in range(2):
                    part = slice(h * 256, (h + 1) * 256)
                    weights = pair[:, part].astype(jnp.float32)
                    inner = jnp.sum(grad_p[:, part] * weights, -1, keepdims=True)
                    parts.append((weights * (grad_p[:, part] - inner)).astype(jnp.bfloat16))
                grad_s = jnp.concatenate(parts, 1)
                back_v = dot_columns(pair, upstream)
                back_k = dot_columns(grad_s, v.projected[row, cols])
                at = slice(k * 128, (k + 1) * 128)
                grad_q = rotate(dot(grad_s, key_pair) * HDIM**-0.5, cosine[at, :], -sine[at, :])
                v.projected[row, cols] = grad_q.astype(jnp.bfloat16)
                for which, back in ((0, back_k), (1, back_v)):
                    back = jnp.where(side, back[:256], back[256:])
                    out = v.second if which == 0 else v.grad_v
                    if k == 0:
                        v.edge[r, 0, which, :, cols] = back[:HALF].astype(jnp.bfloat16)
                        out[r * span : r * span + 192, cols] = back[HALF:]
                    else:
                        out[r * span + 64 : r * span + 192, cols] += back[:128]
                        out[r * span + 192 : (r + 1) * span, cols] = back[128:192]
                        v.edge[r, 1, which, :, cols] = back[192:].astype(jnp.bfloat16)

            if first == 4 and r == 0:
                load(PROBS + k, src.probs.at[1, k], v.probs.at[k])

        return run

    waits = []
    for i in range(8):
        tasks.add(attend_back(i // 4, (i // 2) % 2, 4 * (i % 2)))
        if i % 4 == 3:
            edge, land = v.edge.at[i // 4], v.edge_landed.at[i // 4]
            start, finish = edge_exchange(tasks, sems, n_seq, edge.at[1], land.at[0], edge.at[0], land.at[1])
            tasks.add(start)
            waits.append(finish)
    for r in range(rows):
        tasks.add(waits[r])

    def turn_back(r):
        def run():
            for part, out in ((0, v.second), (1, v.grad_v)):

                @pl.when(z > 0)
                def _():
                    out[r * span : r * span + HALF, :] += v.edge_landed[r, 0, part].astype(jnp.float32)

                @pl.when(z < n_seq - 1)
                def _():
                    at = slice((r + 1) * span - HALF, (r + 1) * span)
                    out[at, :] += v.edge_landed[r, 1, part].astype(jnp.float32)

            @pl.loop(0, 8)
            def _(p):
                at, cols = slice(r * span, (r + 1) * span), tile(p, 128)
                turned = rotate(v.second[at, cols], cosine[...], -sine[...])
                v.projected[at, pl.ds(pl.multiple_of(1024 + p * 128, 128), 128)] = turned.astype(jnp.bfloat16)
                v.projected[at, pl.ds(pl.multiple_of(2048 + p * 128, 128), 128)] = v.grad_v[at, cols].astype(
                    jnp.bfloat16
                )

        return run

    for r in range(rows):
        tasks.add(turn_back(r))

    def grad_qkv(first):
        inner = grad_weight("q", first, 4, lambda cols: v.projected[:, cols])

        def run():
            if first == 0:
                wait(FLIPPED)
            inner()

        return run

    for i, letter in enumerate("abc"):
        tasks.add(grad_qkv(4 * i))

    def grad_normed(i):
        def run():
            wait(WIDE + i % 2)

            @pl.loop(0, 2)
            def _(j):
                block = v.ring[i % 2, j].reshape(512, 1024)
                part = dot_rows(v.projected[:, i * 1024 : (i + 1) * 1024], block)
                if i == 0:
                    v.grad_v[:, tile(j, 512)] = part
                else:
                    v.grad_v[:, tile(j, 512)] += part

            if i == 0:
                load(WIDE, src.q.at[:, :, :, :, pl.ds(2048, 1024)], v.ring.at[0])

        return run

    for i in range(3):
        tasks.add(grad_normed(i))

    def first_norm_back():
        @pl.loop(0, 8)
        def _(i):
            at = tile(i, 64)
            grad = norm_back(tokens[at, :].astype(jnp.float32), v.grad_v[at, :], v.gains[0:1, :])
            v.branch[at, :] = (v.middle[at, :] + grad).astype(jnp.bfloat16)

        load(RESULT, v.branch, grad_tokens)

    tasks.add(first_norm_back)
    if direct:
        sources = dict(others)
        sources.update({n: g.at[1] for n, g in (("n", src.grad_narrow), ("w", src.grad_wide))})
        add_scatter(tasks, SCATTER_STREAMS, SCATTER_CHUNKS, sources, totals, slots, landed, sums, sems, credit)
        load(TOTAL, src.grad_narrow.at[0], totals["n"])
        load(TOTAL + 1, src.grad_wide.at[0], totals["w"])
    load_group(0)
    load_group(1)
    load(MIDDLE, src.middle, v.middle)
    load(GAINS, src.gains, v.gains)
    load(QUERIES, src.queries, v.projected.at[:, pl.ds(0, 1024)])
    load(KEYS, src.keys, v.keys)
    load(VALUES, src.values, v.values)
    load(FLIPPED, src.flip_attended, v.flipped)
    for k in range(2):
        load(PROBS + k, src.probs.at[0, k], v.probs.at[k])
    enter(direct, n_seq)
    if direct:
        wait(TOTAL)
        wait(TOTAL + 1)
    tasks.run(BACKWARD_ORDER if direct else range(len(tasks.steps)))
    if not direct:
        for i, name in enumerate("qo"):
            load(OWN + i, totals[name], sums[i])
            load(OTHER + i, others[name], sums[2 + i])
    for copy in local.values():
        copy.wait()


WIDE, EXPANDED, PROBS, TOTAL, OWN, OTHER = 0, 2, 4, 6, 8, 10
MIDDLE, GAINS, QUERIES, KEYS, VALUES, FLIPPED, RESULT, LOADS = range(12, 20)


def backward(direct, n_seq, saved, *inputs):
    split = lambda a: a.reshape(2, 2, 2, 128, -1)
    saved = saved._replace(grad_narrow=split(saved.grad_narrow), grad_wide=split(saved.grad_wide))
    shapes = landing_shapes(SCATTER_STREAMS) if direct else []
    widths = {"q": 3072, "o": 1024, "w": 2 * PADDED, "n": PADDED}
    held = WEIGHTS if direct else ("q", "o")
    half = lambda n: (2, 2, 128, widths[n])
    if direct:
        sums = [jax.ShapeDtypeStruct((32, widths[n]), F32) for n in WEIGHTS]
    else:
        sums = [jax.ShapeDtypeStruct(half(n), BF) for n in ("q", "o", "q", "o")]
    largest = max(count for _, _, count in SCATTER_CHUNKS)
    count = 400 if direct else 16
    out = pl.pallas_call(
        functools.partial(backward_kernel, direct, n_seq, shapes),
        out_shape=(jax.ShapeDtypeStruct((512, 1024), BF), *sums),
        in_specs=[ANY] * len(saved) + [VMEM] * len(inputs),
        out_specs=(ANY, *([VMEM if direct else ANY] * 4)),
        scratch_shapes=[pltpu.VMEM(half(n), BF) for n in held]
        + [pltpu.VMEM(half(n), BF) for n in ("q", "o")]
        + [pltpu.VMEM(s, BF) for stream in shapes for s in stream.values()]
        + ([pltpu.VMEM((2, 2, 2, 128, largest), BF)] if direct else [])
        + [
            pltpu.VMEM((2, 2, 2, 2, 128, 1024), BF),
            pltpu.VMEM((2, 512, 768), BF),
            pltpu.VMEM((512, 1024), F32),
            pltpu.VMEM((512, 1024), F32),
            pltpu.VMEM((512, 1024), BF),
            pltpu.VMEM((1024, 512), BF),
            pltpu.VMEM((2, 384, 1024), BF),
            pltpu.VMEM((2, 384, 1024), BF),
            pltpu.VMEM((2, 8, 128, 512), BF),
            pltpu.VMEM((512, 3072), BF),
            pltpu.VMEM((512, 1024), F32),
            pltpu.VMEM((2, 2, 2, HALF, 1024), BF),
            pltpu.VMEM((2, 2, 2, HALF, 1024), BF),
            pltpu.VMEM((8, 1024), F32),
            pltpu.SemaphoreType.DMA((count,)),
            pltpu.SemaphoreType.DMA((count,)),
            pltpu.SemaphoreType.DMA((LOADS,)),
            pltpu.SemaphoreType.REGULAR((2,)),
        ],
        compiler_params=pltpu.CompilerParams(collective_id=2, has_side_effects=True, vmem_limit_bytes=63 << 20),
    )(*saved, *inputs)
    return out


def tables(span):
    frequency = ROPE_BASE ** (-(2.0 * jnp.arange(HDIM // 2, dtype=jnp.float32)) / HDIM)
    positions = (lax.axis_index(SEQ) * span + jnp.arange(span, dtype=jnp.int32)).astype(jnp.float32)
    angles = positions[:, None] * frequency[None, :]
    cosine, sine = jnp.cos(angles), jnp.sin(angles)
    return jnp.concatenate([cosine] * 4, 1), jnp.concatenate([-sine, sine, -sine, sine], 1)


def interleave(wide):
    lead = wide.shape[0]
    wide = jnp.pad(wide.reshape(lead, 2, FF), ((0, 0), (0, 0), (0, PADDED - FF)))
    return wide.reshape(lead, 2, PADDED // 128, 128).swapaxes(1, 2).reshape(lead, 2 * PADDED)


def separate(wide):
    lead = wide.shape[0]
    wide = wide.reshape(lead, PADDED // 128, 2, 128).swapaxes(1, 2).reshape(lead, 2, PADDED)
    return wide[:, :, :FF].reshape(lead, 2 * FF)


def body(
    tokens,
    segment_ids,
    padding_mask,
    qkv_weight,
    out_weight,
    wide_weight,
    narrow_weight,
    first_gain,
    second_gain,
    cotangent,
):
    row_count, span, width = tokens.shape
    count = row_count * span
    n_seq = lax.axis_size(SEQ)
    direct = (lax.axis_size(BATCH), n_seq) == (8, 4)
    gains = jnp.stack([first_gain, second_gain], axis=1)
    shards = (
        jnp.pad(gains, ((0, 0), (0, 126))),
        qkv_weight,
        out_weight,
        interleave(wide_weight),
        jnp.pad(narrow_weight, ((0, 0), (0, PADDED - FF))),
    )
    if not direct:
        shards = [
            lax.all_gather(s, (BATCH, SEQ), axis=0, tiled=True).reshape(2, 2, 2, 128, s.shape[-1]) for s in shards
        ]
    tags = jnp.where(padding_mask == 1, segment_ids + 1, 0).astype(jnp.float32)
    tag_center = jnp.pad(tags, ((0, 8 - row_count), (HALF, HALF)))
    tag_edge = jnp.pad(
        jnp.concatenate([tags[:, span - HALF :], tags[:, :HALF]], 1), ((0, 8 - row_count), (0, 0))
    )
    query_tag = (segment_ids + 1).astype(jnp.float32).reshape(count, 1)
    cosine, sine = tables(span)
    hidden, upstream = tokens.reshape(count, width), cotangent.reshape(count, width)
    saved = forward(direct, n_seq, shards, hidden, upstream, cosine, sine, tag_center, tag_edge, query_tag)
    grad_tokens, *sums = backward(direct, n_seq, saved, hidden, upstream, cosine, sine)
    if not direct:
        own_q, own_o, other_q, other_o = sums
        grads = [jnp.stack([own, other]) for own, other in ((own_q, other_q), (own_o, other_o))]
        grads += [saved.grad_wide, saved.grad_narrow]
        sums = []
        for g in grads:
            g = jnp.moveaxis(g.reshape(2, 4, 128, -1), 0, 1).reshape(width, -1)
            sums.append(lax.psum_scatter(g, (BATCH, SEQ), scatter_dimension=0, tiled=True).astype(jnp.float32))
    sum_qkv, sum_out, sum_wide, sum_narrow = sums
    wide_shard = interleave(wide_weight)

    def gain_grad(weight, grad, gain):
        return jnp.sum(weight.astype(jnp.float32) * grad, 1) / gain.astype(jnp.float32)

    return (
        saved.outputs.reshape(tokens.shape),
        grad_tokens.reshape(tokens.shape),
        sum_qkv,
        sum_out,
        separate(sum_wide),
        sum_narrow[:, :FF],
        gain_grad(qkv_weight, sum_qkv, first_gain),
        gain_grad(wide_shard, sum_wide, second_gain),
    )


def solution(mesh):
    placed = (
        P(BATCH, SEQ, None),
        P(BATCH, SEQ),
        P(BATCH, SEQ),
        P((BATCH, SEQ), None),
        P((BATCH, SEQ), None),
        P((BATCH, SEQ), None),
        P((BATCH, SEQ), None),
        P((BATCH, SEQ)),
        P((BATCH, SEQ)),
        P(BATCH, SEQ, None),
    )
    return jax.shard_map(
        body,
        mesh=mesh,
        in_specs=placed,
        out_specs=(
            P(BATCH, SEQ, None),
            P(BATCH, SEQ, None),
            P((BATCH, SEQ), None),
            P((BATCH, SEQ), None),
            P((BATCH, SEQ), None),
            P((BATCH, SEQ), None),
            P((BATCH, SEQ)),
            P((BATCH, SEQ)),
        ),
        check_vma=False,
    )
```

time: 445 us -> 314 us (0.71)
  matrix products: 59.8 us -> 0 us
  local copies, waits for them, and re-layouts: 62.4 us -> 14.6 us
  other arithmetic: 30.7 us -> 7.17 us
    dot_general x8 -> x0, matrix products: 59.8 us -> none  [the longest x1 13 us: body(): jnp.einsum('nf,df->nd', grad_expanded, wide_full, preferred_element_type=...]
    mul x3 -> x0, local copies, waits for them, and re-layouts: 29.3 us -> none  [body(): grad_expanded = slopes * grad_act.reshape(count, PADDED // 128, 1, 128)]
    another operation x7 -> x0, other arithmetic: 16.2 us -> none
    pallas_call x1, Pallas kernels: 137 us -> 152 us  [forward(): pl.pallas_call(functools.partial(forward_kernel, direct, n_seq), out_shap...]
    pallas_call x2 -> x1, Pallas kernels: 147 us -> 137 us  [backward(): pl.pallas_call(functools.partial(backward_kernel, direct, n_seq, shapes),...]
    slice x7 -> x0, local copies, waits for them, and re-layouts: 7.44 us -> none  [the longest x2 1.98 us: body(): owned[0]]
  transfers between devices with their start and end apart: 2 -> 0, of which waited for: 0 -> 0; matrix products, arithmetic and copies ran while one was open for 10% -> 0% of each run, Pallas kernels for 0% -> 0%
where the time goes in v3:
time: 314 us; the launch traced here: 311 us
  Pallas kernels  288 us (92%)
  local copies, waits for them, and re-layouts  14.6 us (5%)
  other arithmetic  7.17 us (2%)
    pallas_call x1, Pallas kernels, forward(): pl.pallas_call(functools.partial(forward_kernel, direct, n_seq), out_shap...  152 us
    pallas_call x1, Pallas kernels, backward(): pl.pallas_call(functools.partial(backward_kernel, direct, n_seq, shapes),...  137 us

profile of v3, /device:TPU:0, one launch (start us, length us, event | category | flops | bytes accessed | tf_op | source)
XLA Modules:
  0.0 311.0 jit_solution(5460836673520858733)
XLA Ops:
  0.6 0.7 pad_maximum_fusion.2
  1.3 0.7 convert_bitcast_fusion
  2.1 0.1 fusion.2
  2.1 0.7 select_maximum_fusion.refs_10_
  2.8 0.1 copy.25
  2.9 0.6 pad.21.refs_0_
  3.5 0.7 pad.24.refs_9_
  4.2 1.6 pad.23.refs_4_
  5.8 0.9 copy.29
  6.6 1.3 reshape.70
  8.0 0.3 pad_bitcast_fusion
  8.3 0.9 reshape.72.refs_3_
  9.2 0.5 fusion
  9.7 1.0 pad_maximum_fusion
  10.7 151.6 %shard_map.161 = (bf16[2,2,2,128,3072]{4,3,2,1,0:T(8,128)(2,1)}, bf16[2,2,2,128,1024]{4,3,2,1,0:T(8,128)(2,1)}, bf16[2,2,2,128,5376]{4,3,2,1,0:T(8,128)(2,1)}, b...) custom-call(bf16[32,128]{1,0:T(8,128)(2,1)} %pad.21.refs_0_, ...), custom_call_target="tpu_custom_call" | custom-call | tf_op jit(solution)/shard_map/pallas_call | solution.py:636
  162.2 0.0 copy-start
  162.2 0.0 copy-start.6
  162.3 0.0 copy-start.3
  162.3 0.0 copy-start.7
  162.3 136.8 %shard_map.162 = (bf16[512,1024]{1,0:T(8,128)(2,1)}, f32[32,3072]{1,0:T(8,128)}, f32[32,1024]{1,0:T(8,128)}, f32[32,5376]{1,0:T(8,128)}, f32[32,2688]{1,0:T(8,128)}) custom-call(bf16[2,2,2,128,3072]{4,3,2,1,0:T(8,128)(2,1)} %get-tuple-element.29.refs_0_, bf16[2,2,2,128,1024]{4,3,2,1,0:T(8,128)(2,1)} %get-tuple-element.30.refs_1_, ...), custom_call_target="tpu_custom_call" | custom-call | tf_op jit(solution)/shard_map/pallas_call | solution.py:1148
  299.0 0.0 copy-start.2
  299.1 1.4 multiply_reduce_fusion
  300.5 0.5 convert_divide_fusion
  301.0 1.1 multiply_reduce_fusion.1
  302.2 0.5 convert_divide_fusion.1
  302.7 1.4 reshape.80
  304.1 1.3 reshape.82
  305.5 2.3 copy.35
  307.7 1.0 copy.36
  308.7 0.7 copy.37
  309.5 0.7 copy.38
  310.1 0.7 copy.39
  (14 shorter events, 0.0 us)
Async XLA Ops:
  162.2 136.9 %copy-start = (bf16[32,5376]{1,0:T(8,128)(2,1)S(1)}, bf16[32,5376]{1,0:T(8,128)(2,1)}, u32[]{:S(2)}) copy-start(bf16[32,5376]{1,0:T(8,128)(2,1)} %reshape.72.refs_3_) | copy-start | bytes 1032196
  162.2 138.3 %copy-start.6 = (bf16[32]{0:T(256)(128)(2,1)S(1)}, bf16[32]{0:T(256)(128)(2,1)}, u32[]{:S(2)}) copy-start(bf16[32]{0:T(256)(128)(2,1)} %param.18) | copy-start | bytes 196
  162.3 138.8 %copy-start.3 = (bf16[32,3072]{1,0:T(8,128)(2,1)S(1)}, bf16[32,3072]{1,0:T(8,128)(2,1)}, u32[]{:S(2)}) copy-start(bf16[32,3072]{1,0:T(8,128)(2,1)} %refs_1_.1) | copy-start | bytes 589828
  162.3 139.9 %copy-start.7 = (bf16[32]{0:T(256)(128)(2,1)S(1)}, bf16[32]{0:T(256)(128)(2,1)}, u32[]{:S(2)}) copy-start(bf16[32]{0:T(256)(128)(2,1)} %param.17) | copy-start | bytes 196
  299.0 8.7 %copy-start.2 = (bf16[512,1024]{1,0:T(8,128)(2,1)S(1)}, bf16[512,1024]{1,0:T(8,128)(2,1)}, u32[]{:S(2)}) copy-start(bf16[512,1024]{1,0:T(8,128)(2,1)} %get-tuple-element.43) | copy-start | bytes 3145732
  299.1 9.7 %copy-start.1 = (f32[32,3072]{1,0:T(8,128)S(1)}, f32[32,3072]{1,0:T(8,128)}, u32[]{:S(2)}) copy-start(f32[32,3072]{1,0:T(8,128)} %get-tuple-element.67) | copy-start | bytes 1179652
  299.1 10.4 %copy-start.5 = (f32[32,1024]{1,0:T(8,128)S(1)}, f32[32,1024]{1,0:T(8,128)}, u32[]{:S(2)}) copy-start(f32[32,1024]{1,0:T(8,128)} %get-tuple-element.68) | copy-start | bytes 393220
  299.1 11.0 %copy-start.4 = (f32[32,2688]{1,0:T(8,128)S(1)}, f32[32,2688]{1,0:T(8,128)}, u32[]{:S(2)}) copy-start(f32[32,2688]{1,0:T(8,128)} %get-tuple-element.47) | copy-start | bytes 1032196
